TPU v7x, 128 devices: a whole 4x4x4 slice. The times are simulated.
128 devices in a mesh: section: 2 (over y_lo), gx: 8 (over x, y_hi), gy: 8 (over z, core).
Axes of the slice: x: 4, y: 4 (y_hi: 2, y_lo: 2; y = y_hi * 2 + y_lo), z: 4, core: 2. Of those that a mesh axis runs over, the one named last changes fastest.
Arguments:
- images: bfloat16 [2, 2, 640, 1024], P(None, None, 'gx', 'gy'), may hold values from -6 to 6
- counts: int32 [2], replicated, may hold values from 1 to 2, as said below
- attn_gain: float32 [2, 1024], P('section', 'gy'), may hold values from 0.5 to 1.5
- attn_shift: float32 [2, 1024], P('section', 'gy'), may hold values from -1.75 to 1.75
- w_query: bfloat16 [2, 1024, 1024], P('section', 'gx', 'gy'), may hold values from -0.1875 to 0.1875
- b_query: float32 [2, 1024], P('section', 'gy'), may hold values from -1.75 to 1.75
- w_key: bfloat16 [2, 1024, 1024], P('section', 'gx', 'gy'), may hold values from -0.1875 to 0.1875
- w_value: bfloat16 [2, 1024, 1024], P('section', 'gx', 'gy'), may hold values from -0.1875 to 0.1875
- b_value: float32 [2, 1024], P('section', 'gy'), may hold values from -1.75 to 1.75
- w_out: bfloat16 [2, 1024, 1024], P('section', 'gy', 'gx'), may hold values from -1 to 1
- b_out: float32 [2, 1024], P('section', 'gy'), may hold values from -1.75 to 1.75
- mlp_gain: float32 [2, 1024], P('section', 'gy'), may hold values from 0.5 to 1.5
- mlp_shift: float32 [2, 1024], P('section', 'gy'), may hold values from -1.75 to 1.75
- w_up: bfloat16 [2, 1024, 4096], P('section', 'gx', 'gy'), may hold values from -0.1875 to 0.1875
- b_up: float32 [2, 4096], P('section', 'gy'), may hold values from -1.75 to 1.75
- w_down: bfloat16 [2, 4096, 1024], P('section', 'gy', 'gx'), may hold values from -0.09375 to 0.09375
- b_down: float32 [2, 1024], P('section', 'gy'), may hold values from -1.75 to 1.75
- cotangent: bfloat16 [2, 2, 640, 1024], P(None, None, 'gx', 'gy'), may hold values from -6 to 6
Outputs:
- activations: bfloat16 [2, 2, 2, 640, 1024], P('section', None, None, 'gx', 'gy')
- input_grads: float32 [2, 2, 2, 640, 1024], P('section', None, None, 'gx', 'gy')
- grad_attn_gain: float32 [2, 1024], P('section', 'gy')
- grad_attn_shift: float32 [2, 1024], P('section', 'gy')
- grad_w_query: float32 [2, 1024, 1024], P('section', 'gx', 'gy')
- grad_b_query: float32 [2, 1024], P('section', 'gy')
- grad_w_key: float32 [2, 1024, 1024], P('section', 'gx', 'gy')
- grad_w_value: float32 [2, 1024, 1024], P('section', 'gx', 'gy')
- grad_b_value: float32 [2, 1024], P('section', 'gy')
- grad_w_out: float32 [2, 1024, 1024], P('section', 'gy', 'gx')
- grad_b_out: float32 [2, 1024], P('section', 'gy')
- grad_mlp_gain: float32 [2, 1024], P('section', 'gy')
- grad_mlp_shift: float32 [2, 1024], P('section', 'gy')
- grad_w_up: float32 [2, 1024, 4096], P('section', 'gx', 'gy')
- grad_b_up: float32 [2, 4096], P('section', 'gy')
- grad_w_down: float32 [2, 4096, 1024], P('section', 'gy', 'gx')
- grad_b_down: float32 [2, 1024], P('section', 'gy')
Inputs may be any that keep to these rules, and one draw needn't show every extreme that they name: `counts`: each micro-batch holds 1 to 2 images in its first slots; some micro-batch holds 2.
All inputs are finite; a program needn't handle non-finite values.
Results may differ from a plain program's by a relative error of at most 0.02.
Values may be sent and summed in bfloat16 or wider, within the bound.
A program may use at most 128 MiB of HBM per device.

v0:
```python
import jax
import jax.numpy as jnp
from jax import lax
from jax.sharding import PartitionSpec as P

DH = 64
SEQ = 577


EPSILON = 1e-06


def shifted(array, axis, by):
    peers = lax.axis_size(axis)
    pairs = [(i, i + by) for i in range(peers) if 0 <= i + by < peers]
    return lax.ppermute(array, axis, pairs)


def contract(pattern, left_side, right_side):
    return jnp.einsum(pattern, left_side, right_side, preferred_element_type=jnp.float32)


def fetch_blocks(own_blocks):
    return (
        lax.all_gather(own_blocks[0], "gx", axis=0, tiled=True),
        lax.all_gather(own_blocks[1], "gx", axis=0, tiled=True),
        lax.all_gather(own_blocks[2], "gx", axis=0, tiled=True),
        lax.all_gather(own_blocks[3], "gx", axis=1, tiled=True),
        lax.all_gather(own_blocks[4], "gx", axis=0, tiled=True),
        lax.all_gather(own_blocks[5], "gx", axis=1, tiled=True),
    )


def row_moments(values):
    summed = jnp.sum(values, axis=-1)
    square = jnp.sum(values * values, axis=-1)
    summed, square = lax.psum((summed, square), "gy")
    full_width = values.shape[-1] * lax.axis_size("gy")
    center = summed / full_width
    spread = square / full_width - center * center
    return (center[..., None], lax.rsqrt(spread + EPSILON)[..., None])


def normalize(values, gain_row, shift_row):
    center, scaled = row_moments(values)
    unit_rows = (values - center) * scaled
    normed = (unit_rows * gain_row + shift_row).astype(jnp.bfloat16)
    return (lax.all_gather(normed, "gy", axis=2, tiled=True), unit_rows, scaled)


def norm_backward(grad_normed, unit_rows, scaled, gain_row):
    grad_gain = jnp.sum(grad_normed * unit_rows, axis=(0, 1))
    grad_shift = jnp.sum(grad_normed, axis=(0, 1))
    grad_unit = grad_normed * gain_row
    first_sum = jnp.sum(grad_unit, axis=-1)
    second_sum = jnp.sum(grad_unit * unit_rows, axis=-1)
    first_sum, second_sum = lax.psum((first_sum, second_sum), "gy")
    full_width = unit_rows.shape[-1] * lax.axis_size("gy")
    grad_input = scaled * (
        grad_unit
        - first_sum[..., None] / full_width
        - unit_rows * second_sum[..., None] / full_width
    )
    return (grad_input, grad_gain, grad_shift)


def sum_branch(partial_rows):
    return lax.psum_scatter(
        partial_rows.astype(jnp.bfloat16), "gy", scatter_dimension=2, tiled=True
    ).astype(jnp.float32)


def gather_grad(values):
    return lax.all_gather(values.astype(jnp.bfloat16), "gy", axis=2, tiled=True)


def sum_features(partial_rows):
    return lax.psum_scatter(
        partial_rows.astype(jnp.bfloat16), "gy", scatter_dimension=2, tiled=True
    ).astype(jnp.float32)


def split_heads(values):
    return values.reshape(values.shape[0], values.shape[1], values.shape[2] // DH, DH)


def score_rows(query_heads, key_heads):
    scores = contract("cqhd,ckhd->chqk", query_heads, key_heads) * DH ** (-0.5)
    key_valid = jnp.arange(key_heads.shape[1]) < SEQ
    return jnp.where(key_valid[None, None, None, :], scores, -1e30)


def exact_gelu(values):
    return jax.nn.gelu(values, approximate=False)


def forward_layer(inputs, vectors, blocks):
    attn_gain, attn_shift, b_query, b_value, b_out, mlp_gain, mlp_shift, b_up, b_down = vectors
    w_query, w_key, w_value, w_out, w_up, w_down = blocks
    normed, unit_one, scaled_one = normalize(inputs, attn_gain, attn_shift)
    queries = (contract("csd,de->cse", normed, w_query) + b_query).astype(jnp.bfloat16)
    key_part = contract("csd,de->cse", normed, w_key).astype(jnp.bfloat16)
    value_part = (contract("csd,de->cse", normed, w_value) + b_value).astype(jnp.bfloat16)
    key_rows, value_rows = (
        lax.all_gather(key_part, "gx", axis=1, tiled=True),
        lax.all_gather(value_part, "gx", axis=1, tiled=True),
    )
    masked = score_rows(split_heads(queries), split_heads(key_rows))
    highest = jnp.max(masked, axis=-1, keepdims=True)
    exponent = jnp.exp(masked - highest)
    summed = jnp.sum(exponent, axis=-1, keepdims=True)
    weights = (exponent / summed).astype(jnp.bfloat16)
    log_summed = highest + jnp.log(summed)
    mixed_heads = contract("chqk,ckhd->cqhd", weights, split_heads(value_rows)).astype(jnp.bfloat16)
    mixed_heads = mixed_heads.reshape(queries.shape)
    middle = inputs + sum_branch(contract("cse,ef->csf", mixed_heads, w_out)) + b_out
    normed_two, unit_two, scaled_two = normalize(middle, mlp_gain, mlp_shift)
    hidden_pre = contract("csd,de->cse", normed_two, w_up) + b_up
    hidden = exact_gelu(hidden_pre).astype(jnp.bfloat16)
    output = middle + sum_branch(contract("cse,ef->csf", hidden, w_down)) + b_down
    stored = (
        normed,
        unit_one,
        scaled_one,
        queries,
        key_rows,
        value_rows,
        log_summed,
        mixed_heads,
        normed_two,
        unit_two,
        scaled_two,
        hidden_pre,
        hidden,
    )
    return (output, stored)


def backward_layer(grad_output, stored, vectors, blocks):
    attn_gain, attn_shift, b_query, b_value, b_out, mlp_gain, mlp_shift, b_up, b_down = vectors
    w_query, w_key, w_value, w_out, w_up, w_down = blocks
    (
        normed,
        unit_one,
        scaled_one,
        queries,
        key_rows,
        value_rows,
        log_summed,
        mixed_heads,
        normed_two,
        unit_two,
        scaled_two,
        hidden_pre,
        hidden,
    ) = stored
    grad_down_b = jnp.sum(grad_output, axis=(0, 1))
    grad_full = gather_grad(grad_output)
    grad_w_down = contract("cse,csf->ef", hidden, grad_full)
    grad_hidden = contract("csf,ef->cse", grad_full, w_down)
    gelu_value, gelu_back = jax.vjp(exact_gelu, hidden_pre)
    grad_pre = gelu_back(grad_hidden)[0].astype(jnp.bfloat16)
    grad_up_b = jnp.sum(grad_pre.astype(jnp.float32), axis=(0, 1))
    grad_w_up = contract("csd,cse->de", normed_two, grad_pre)
    grad_normed_two = sum_features(contract("cse,de->csd", grad_pre, w_up))
    grad_norm_two, grad_mlp_gain, grad_mlp_shift = norm_backward(
        grad_normed_two, unit_two, scaled_two, mlp_gain
    )
    grad_middle = grad_output + grad_norm_two
    grad_out_b = jnp.sum(grad_middle, axis=(0, 1))
    middle_full = gather_grad(grad_middle)
    grad_w_out = contract("cse,csf->ef", mixed_heads, middle_full)
    grad_mixed = split_heads(contract("csf,ef->cse", middle_full, w_out).astype(jnp.bfloat16))
    query_heads = split_heads(queries)
    key_heads = split_heads(key_rows)
    value_heads = split_heads(value_rows)
    masked = score_rows(query_heads, key_heads)
    weights_full = jnp.exp(masked - log_summed)
    weights = weights_full.astype(jnp.bfloat16)
    grad_weights = contract("cqhd,ckhd->chqk", grad_mixed, value_heads)
    inner_sum = jnp.sum(grad_weights * weights_full, axis=-1, keepdims=True)
    grad_scores = (weights_full * (grad_weights - inner_sum)).astype(jnp.bfloat16)
    scale_factor = DH ** (-0.5)
    grad_query = (
        (contract("chqk,ckhd->cqhd", grad_scores, key_heads) * scale_factor)
        .astype(jnp.bfloat16)
        .reshape(queries.shape)
    )
    grad_value = contract("chqk,cqhd->ckhd", weights, grad_mixed)
    grad_key = contract("chqk,cqhd->ckhd", grad_scores, query_heads) * scale_factor
    grad_key, grad_value = (
        lax.psum_scatter(
            grad_key.reshape(key_rows.shape).astype(jnp.bfloat16),
            "gx",
            scatter_dimension=1,
            tiled=True,
        ).astype(jnp.float32),
        lax.psum_scatter(
            grad_value.reshape(value_rows.shape).astype(jnp.bfloat16),
            "gx",
            scatter_dimension=1,
            tiled=True,
        ).astype(jnp.float32),
    )
    grad_key = grad_key.astype(jnp.bfloat16)
    grad_value = grad_value.astype(jnp.bfloat16)
    grad_query_b = jnp.sum(grad_query.astype(jnp.float32), axis=(0, 1))
    grad_value_b = jnp.sum(grad_value.astype(jnp.float32), axis=(0, 1))
    grad_w_query = contract("csd,cse->de", normed, grad_query)
    grad_w_key = contract("csd,cse->de", normed, grad_key)
    grad_w_value = contract("csd,cse->de", normed, grad_value)
    grad_normed = (
        contract("cse,de->csd", grad_query, w_query)
        + contract("cse,de->csd", grad_key, w_key)
        + contract("cse,de->csd", grad_value, w_value)
    )
    grad_normed = sum_features(grad_normed)
    grad_norm_one, grad_attn_gain, grad_attn_shift = norm_backward(
        grad_normed, unit_one, scaled_one, attn_gain
    )
    grad_inputs = grad_middle + grad_norm_one
    vector_grads = (
        grad_attn_gain,
        grad_attn_shift,
        grad_query_b,
        grad_value_b,
        grad_out_b,
        grad_mlp_gain,
        grad_mlp_shift,
        grad_up_b,
        grad_down_b,
    )
    block_grads = (grad_w_query, grad_w_key, grad_w_value, grad_w_out, grad_w_up, grad_w_down)
    return (grad_inputs, vector_grads, block_grads)


def place_micro(buffer, value, slot_index):
    valid = (slot_index >= 0) & (slot_index < buffer.shape[0])
    clipped = jnp.clip(slot_index, 0, buffer.shape[0] - 1)
    updated = lax.dynamic_update_index_in_dim(buffer, value, clipped, 0)
    return jnp.where(valid, updated, buffer)


def local(
    images,
    counts,
    attn_gain,
    attn_shift,
    w_query,
    b_query,
    w_key,
    w_value,
    b_value,
    w_out,
    b_out,
    mlp_gain,
    mlp_shift,
    w_up,
    b_up,
    w_down,
    b_down,
    cotangent,
):
    section_no = lax.axis_index("section")
    vectors = (
        attn_gain[0],
        attn_shift[0],
        b_query[0],
        b_value[0],
        b_out[0],
        mlp_gain[0],
        mlp_shift[0],
        b_up[0],
        b_down[0],
    )
    own_blocks = (w_query[0], w_key[0], w_value[0], w_out[0], w_up[0], w_down[0])
    held_blocks = fetch_blocks(own_blocks)
    micro_count = images.shape[0]
    last_micro = micro_count - 1
    activations = jnp.zeros(images.shape, jnp.bfloat16)
    received = jnp.zeros(images.shape[1:], jnp.bfloat16)
    stored_all = []
    for time_step in range(micro_count + 1):
        blocks = held_blocks
        own_input = images[min(time_step, last_micro)]
        inputs = jnp.where(section_no == 0, own_input, received).astype(jnp.float32)
        output, stored = forward_layer(inputs, vectors, blocks)
        sending = output.astype(jnp.bfloat16)
        activations = place_micro(activations, sending, time_step - section_no)
        stored_all.append(stored)
        received = shifted(sending, "section", 1)
    positions = lax.axis_index("gx") * images.shape[2] + jnp.arange(images.shape[2])
    position_ok = positions < SEQ
    image_ids = jnp.arange(images.shape[1])
    input_grads = jnp.zeros(images.shape, jnp.float32)
    returned = jnp.zeros(images.shape[1:], jnp.float32)
    vector_sums = tuple((jnp.zeros(item.shape, jnp.float32) for item in vectors))
    block_sums = None
    for time_step in range(micro_count + 1):
        if time_step < micro_count:
            index_back = last_micro - time_step
            rows_ok = (image_ids[:, None] < counts[index_back]) & position_ok[None, :]
            seed_grad = cotangent[index_back].astype(jnp.float32) * rows_ok[:, :, None].astype(
                jnp.float32
            )
        else:
            seed_grad = jnp.zeros(returned.shape, jnp.float32)
        grad_here = jnp.where(section_no == 1, seed_grad, returned)
        blocks = held_blocks
        grad_inputs, vector_grads, block_grads = backward_layer(
            grad_here, stored_all[micro_count - time_step], vectors, blocks
        )
        vector_sums = tuple((acc + new for acc, new in zip(vector_sums, vector_grads)))
        if block_sums is None:
            block_sums = block_grads
        else:
            block_sums = tuple((acc + new for acc, new in zip(block_sums, block_grads)))
        input_grads = place_micro(input_grads, grad_inputs, last_micro - time_step + 1 - section_no)
        returned = shifted(grad_inputs.astype(jnp.bfloat16), "section", -1).astype(jnp.float32)
    block_final = (
        lax.psum_scatter(
            block_sums[0].astype(jnp.bfloat16), "gx", scatter_dimension=0, tiled=True
        ).astype(jnp.float32),
        lax.psum_scatter(
            block_sums[1].astype(jnp.bfloat16), "gx", scatter_dimension=0, tiled=True
        ).astype(jnp.float32),
        lax.psum_scatter(
            block_sums[2].astype(jnp.bfloat16), "gx", scatter_dimension=0, tiled=True
        ).astype(jnp.float32),
        lax.psum_scatter(
            block_sums[3].astype(jnp.bfloat16), "gx", scatter_dimension=1, tiled=True
        ).astype(jnp.float32),
        lax.psum_scatter(
            block_sums[4].astype(jnp.bfloat16), "gx", scatter_dimension=0, tiled=True
        ).astype(jnp.float32),
        lax.psum_scatter(
            block_sums[5].astype(jnp.bfloat16), "gx", scatter_dimension=1, tiled=True
        ).astype(jnp.float32),
    )
    vector_final = lax.psum(vector_sums, "gx")
    return (
        activations[None],
        input_grads[None],
        vector_final[0][None],
        vector_final[1][None],
        block_final[0][None],
        vector_final[2][None],
        block_final[1][None],
        block_final[2][None],
        vector_final[3][None],
        block_final[3][None],
        vector_final[4][None],
        vector_final[5][None],
        vector_final[6][None],
        block_final[4][None],
        vector_final[7][None],
        block_final[5][None],
        vector_final[8][None],
    )


def solution(mesh):
    in_specs = (
        P(None, None, "gx", "gy"),
        P(),
        P("section", "gy"),
        P("section", "gy"),
        P("section", "gx", "gy"),
        P("section", "gy"),
        P("section", "gx", "gy"),
        P("section", "gx", "gy"),
        P("section", "gy"),
        P("section", "gy", "gx"),
        P("section", "gy"),
        P("section", "gy"),
        P("section", "gy"),
        P("section", "gx", "gy"),
        P("section", "gy"),
        P("section", "gy", "gx"),
        P("section", "gy"),
        P(None, None, "gx", "gy"),
    )
    out_specs = (
        P("section", None, None, "gx", "gy"),
        P("section", None, None, "gx", "gy"),
        P("section", "gy"),
        P("section", "gy"),
        P("section", "gx", "gy"),
        P("section", "gy"),
        P("section", "gx", "gy"),
        P("section", "gx", "gy"),
        P("section", "gy"),
        P("section", "gy", "gx"),
        P("section", "gy"),
        P("section", "gy"),
        P("section", "gy"),
        P("section", "gx", "gy"),
        P("section", "gy"),
        P("section", "gy", "gx"),
        P("section", "gy"),
    )
    return jax.shard_map(local, mesh=mesh, in_specs=in_specs, out_specs=out_specs, check_vma=False)
```

profile of v0, /device:TPU:1, one launch (start us, length us, event | category | flops | bytes accessed | tf_op | source)
XLA Modules:
  0.0 2050.1 jit_solution(1347484775613994767)
XLA Ops:
  9.9 14.5 all-reduce.11
  39.7 28.4 %all-gather = bf16[1,1024,128]{2,1,0:T(8,128)(2,1)S(1)} all-gather(bf16[1,128,128]{2,1,0:T(8,128)(2,1)} %param.25), channel_id=2, replica_groups=mesh['section'=2,'gx'=8,'gy'=8] {'gx'}, dimensions={1}, use_global_device_ids=true | all-gather | bytes 294912 | tf_op jit(solution)/shard_map/all_gather | solution.py:27
  69.0 28.9 %all_gather.74 = bf16[2,640,128]{2,1,0:T(8,128)(2,1)S(1)} all-gather(bf16[2,80,128]{2,1,0:T(8,128)(2,1)S(1)} %fusion.26), channel_id=1, replica_groups=mesh['section'=2,'gx'=8,'gy'=8] {'gx'}, dimensions={1}, use_global_device_ids=true | all-gather | bytes 368640 | tf_op jit(solution)/shard_map/all_gather | solution.py:106
  98.2 28.1 %all-gather.1 = bf16[1,1024,128]{2,1,0:T(8,128)(2,1)S(1)} all-gather(bf16[1,128,128]{2,1,0:T(8,128)(2,1)S(1)} %copy-done.107), channel_id=3, replica_groups=mesh['section'=2,'gx'=8,'gy'=8] {'gx'}, dimensions={1}, use_global_device_ids=true | all-gather | bytes 294912 | tf_op jit(solution)/shard_map/all_gather | solution.py:25
  126.7 28.5 %all-gather.2 = bf16[1,1024,128]{2,1,0:T(8,128)(2,1)S(1)} all-gather(bf16[1,128,128]{2,1,0:T(8,128)(2,1)S(1)} %copy-done.108), channel_id=4, replica_groups=mesh['section'=2,'gx'=8,'gy'=8] {'gx'}, dimensions={1}, use_global_device_ids=true | all-gather | bytes 294912 | tf_op jit(solution)/shard_map/all_gather | solution.py:26
  155.4 28.6 %all_gather.77 = bf16[2,640,128]{2,1,0:T(8,128)(2,1)S(1)} all-gather(bf16[2,80,128]{2,1,0:T(8,128)(2,1)S(1)} %convolution_convert_fusion.20), channel_id=1, replica_groups=mesh['section'=2,'gx'=8,'gy'=8] {'gx'}, dimensions={1}, use_global_device_ids=true | all-gather | bytes 368640 | tf_op jit(solution)/shard_map/all_gather | solution.py:105
  184.2 25.9 %all-gather.3 = bf16[1,128,1024]{2,1,0:T(8,128)(2,1)S(1)} all-gather(bf16[1,128,128]{2,1,0:T(8,128)(2,1)S(1)} %copy-done.109), channel_id=5, replica_groups=mesh['section'=2,'gx'=8,'gy'=8] {'gx'}, dimensions={2}, use_global_device_ids=true | all-gather | bytes 294912 | tf_op jit(solution)/shard_map/all_gather | solution.py:28
  214.9 61.4 %reduce-scatter.73.cloned.1.call-done = bf16[128,160]{1,0:T(8,128)(2,1)} async-done(((bf16[1024,160]{1,0:T(8,128)(2,1)}), bf16[128,160]{1,0:T(8,128)(2,1)}) %reduce-scatter.73.cloned.1.call-update) | async-done | bytes 40976
  277.5 15.8 all-reduce.10
  307.5 38.1 %all-gather.11.cloned.1.call-done = bf16[1,512,1024]{2,1,0:T(8,128)(2,1)} async-done(((bf16[1,512,128]{2,1,0:T(8,128)(2,1)}), bf16[1,512,1024]{2,1,0:T(8,128)(2,1)}) %all-gather.11.cloned.1.call-update) | async-done | bytes 1048592 | tf_op jit(solution)/shard_map/all_gather | solution.py:30
  351.1 29.0 %reduce-scatter.75.cloned.1.call-done = bf16[128,160]{1,0:T(8,128)(2,1)} async-done(((bf16[1024,160]{1,0:T(8,128)(2,1)}), bf16[128,160]{1,0:T(8,128)(2,1)}) %reduce-scatter.75.cloned.1.call-update) | async-done | bytes 40976
  385.6 16.1 all-reduce.9
  414.7 28.7 %all_gather.83 = bf16[2,640,128]{2,1,0:T(8,128)(2,1)S(1)} all-gather(bf16[2,80,128]{2,1,0:T(8,128)(2,1)S(1)} %fusion.28), channel_id=1, replica_groups=mesh['section'=2,'gx'=8,'gy'=8] {'gx'}, dimensions={1}, use_global_device_ids=true | all-gather | bytes 368640 | tf_op jit(solution)/shard_map/all_gather | solution.py:106
  444.4 28.5 %all_gather.84 = bf16[2,640,128]{2,1,0:T(8,128)(2,1)S(1)} all-gather(bf16[2,80,128]{2,1,0:T(8,128)(2,1)S(1)} %convolution_convert_fusion.19), channel_id=1, replica_groups=mesh['section'=2,'gx'=8,'gy'=8] {'gx'}, dimensions={1}, use_global_device_ids=true | all-gather | bytes 368640 | tf_op jit(solution)/shard_map/all_gather | solution.py:105
  482.1 40.8 %reduce-scatter.77.cloned.1.call-done = bf16[128,160]{1,0:T(8,128)(2,1)} async-done(((bf16[1024,160]{1,0:T(8,128)(2,1)}), bf16[128,160]{1,0:T(8,128)(2,1)}) %reduce-scatter.77.cloned.1.call-update) | async-done | bytes 40976
  524.2 15.4 all-reduce.8
  561.0 27.8 %reduce-scatter.79.cloned.1.call-done = bf16[128,160]{1,0:T(8,128)(2,1)} async-done(((bf16[1024,160]{1,0:T(8,128)(2,1)}), bf16[128,160]{1,0:T(8,128)(2,1)}) %reduce-scatter.79.cloned.1.call-update) | async-done | bytes 40976
  598.1 15.6 all-reduce.7
  628.5 28.7 %all_gather.87 = bf16[2,640,128]{2,1,0:T(8,128)(2,1)S(1)} all-gather(bf16[2,80,128]{2,1,0:T(8,128)(2,1)S(1)} %fusion.30), channel_id=1, replica_groups=mesh['section'=2,'gx'=8,'gy'=8] {'gx'}, dimensions={1}, use_global_device_ids=true | all-gather | bytes 368640 | tf_op jit(solution)/shard_map/all_gather | solution.py:106
  659.6 28.5 %all_gather.88 = bf16[2,640,128]{2,1,0:T(8,128)(2,1)S(1)} all-gather(bf16[2,80,128]{2,1,0:T(8,128)(2,1)S(1)} %convolution_convert_fusion.18), channel_id=1, replica_groups=mesh['section'=2,'gx'=8,'gy'=8] {'gx'}, dimensions={1}, use_global_device_ids=true | all-gather | bytes 368640 | tf_op jit(solution)/shard_map/all_gather | solution.py:105
  700.2 24.7 %all_gather.90 = bf16[2,80,1024]{2,1,0:T(8,128)(2,1)} all-gather(bf16[2,80,128]{2,1,0:T(8,128)(2,1)S(1)} %fusion.192), channel_id=1, replica_groups=mesh['section'=2,'gx'=8,'gy'=8] {'gy'}, dimensions={2}, use_global_device_ids=true | all-gather | bytes 368640 | tf_op jit(solution)/shard_map/all_gather | solution.py:74
  743.1 16.1 all-reduce.6
  783.6 27.8 %reduce-scatter.85.cloned.1.call-done = bf16[128,160]{1,0:T(8,128)(2,1)} async-done(((bf16[1024,160]{1,0:T(8,128)(2,1)}), bf16[128,160]{1,0:T(8,128)(2,1)}) %reduce-scatter.85.cloned.1.call-update) | async-done | bytes 40976
  816.1 16.1 all-reduce.5
  864.8 53.4 %reduce-scatter.53.cloned.1.call-done = bf16[2,80,128]{2,1,0:T(8,128)(2,1)} async-done(((bf16[2,640,128]{2,1,0:T(8,128)(2,1)}), bf16[2,80,128]{2,1,0:T(8,128)(2,1)}) %reduce-scatter.53.cloned.1.call-update) | async-done | bytes 40976 | tf_op jit(solution)/shard_map/reduce_scatter | solution.py:192
  920.4 64.4 %reduce-scatter.55.cloned.1.call-done = bf16[2,80,128]{2,1,0:T(8,128)(2,1)} async-done(((bf16[2,640,128]{2,1,0:T(8,128)(2,1)}), bf16[2,80,128]{2,1,0:T(8,128)(2,1)}) %reduce-scatter.55.cloned.1.call-update) | async-done | bytes 40976 | tf_op jit(solution)/shard_map/reduce_scatter | solution.py:198
  991.1 29.7 %reduce-scatter.87.cloned.1.call-done = bf16[128,160]{1,0:T(8,128)(2,1)} async-done(((bf16[1024,160]{1,0:T(8,128)(2,1)}), bf16[128,160]{1,0:T(8,128)(2,1)}) %reduce-scatter.87.cloned.1.call-update) | async-done | bytes 40976
  1022.5 15.3 all-reduce.4
  1066.2 28.5 %reduce-scatter.89.cloned.1.call-done = bf16[128,160]{1,0:T(8,128)(2,1)} async-done(((bf16[1024,160]{1,0:T(8,128)(2,1)}), bf16[128,160]{1,0:T(8,128)(2,1)}) %reduce-scatter.89.cloned.1.call-update) | async-done | bytes 40976
  1099.3 15.3 all-reduce.3
  1145.7 53.6 %reduce-scatter.57.cloned.1.call-done = bf16[2,80,128]{2,1,0:T(8,128)(2,1)} async-done(((bf16[2,640,128]{2,1,0:T(8,128)(2,1)}), bf16[2,80,128]{2,1,0:T(8,128)(2,1)}) %reduce-scatter.57.cloned.1.call-update) | async-done | bytes 40976 | tf_op jit(solution)/shard_map/reduce_scatter | solution.py:192
  1200.6 65.2 %reduce-scatter.59.cloned.1.call-done = bf16[2,80,128]{2,1,0:T(8,128)(2,1)} async-done(((bf16[2,640,128]{2,1,0:T(8,128)(2,1)}), bf16[2,80,128]{2,1,0:T(8,128)(2,1)}) %reduce-scatter.59.cloned.1.call-update) | async-done | bytes 40976 | tf_op jit(solution)/shard_map/reduce_scatter | solution.py:198
  1270.1 29.8 %reduce-scatter.91.cloned.1.call-done = bf16[128,160]{1,0:T(8,128)(2,1)} async-done(((bf16[1024,160]{1,0:T(8,128)(2,1)}), bf16[128,160]{1,0:T(8,128)(2,1)}) %reduce-scatter.91.cloned.1.call-update) | async-done | bytes 40976
  1301.6 15.4 all-reduce.2
  1342.4 28.5 %reduce-scatter.93.cloned.1.call-done = bf16[128,160]{1,0:T(8,128)(2,1)} async-done(((bf16[1024,160]{1,0:T(8,128)(2,1)}), bf16[128,160]{1,0:T(8,128)(2,1)}) %reduce-scatter.93.cloned.1.call-update) | async-done | bytes 40976
  1372.7 15.4 all-reduce.1
  1421.1 45.8 %reduce-scatter.61.cloned.1.call-done = bf16[2,80,128]{2,1,0:T(8,128)(2,1)} async-done(((bf16[2,640,128]{2,1,0:T(8,128)(2,1)}), bf16[2,80,128]{2,1,0:T(8,128)(2,1)}) %reduce-scatter.61.cloned.1.call-update) | async-done | bytes 40976 | tf_op jit(solution)/shard_map/reduce_scatter | solution.py:192
  1469.6 63.9 %reduce-scatter.63.cloned.1.call-done = bf16[2,80,128]{2,1,0:T(8,128)(2,1)} async-done(((bf16[2,640,128]{2,1,0:T(8,128)(2,1)}), bf16[2,80,128]{2,1,0:T(8,128)(2,1)}) %reduce-scatter.63.cloned.1.call-update) | async-done | bytes 40976 | tf_op jit(solution)/shard_map/reduce_scatter | solution.py:198
  1545.2 20.1 reduce-scatter.83.cloned.1.call-done
  1570.0 69.1 %reduce-scatter.97.cloned.1.call-done = bf16[128,128]{1,0:T(8,128)(2,1)} async-done(((bf16[1024,128]{1,0:T(8,128)(2,1)}), bf16[128,128]{1,0:T(8,128)(2,1)}) %reduce-scatter.97.cloned.1.call-update) | async-done | bytes 32784
  1640.6 71.8 %reduce-scatter.65.cloned.1.call-done = bf16[128,128]{1,0:T(8,128)(2,1)} async-done(((bf16[1024,128]{1,0:T(8,128)(2,1)}), bf16[128,128]{1,0:T(8,128)(2,1)}) %reduce-scatter.65.cloned.1.call-update) | async-done | bytes 32784 | tf_op jit(solution)/shard_map/reduce_scatter | solution.py:321
  1713.8 71.8 %reduce-scatter.67.cloned.1.call-done = bf16[128,128]{1,0:T(8,128)(2,1)} async-done(((bf16[1024,128]{1,0:T(8,128)(2,1)}), bf16[128,128]{1,0:T(8,128)(2,1)}) %reduce-scatter.67.cloned.1.call-update) | async-done | bytes 32784 | tf_op jit(solution)/shard_map/reduce_scatter | solution.py:324
  1787.0 71.3 %reduce-scatter.69.cloned.1.call-done = bf16[128,128]{1,0:T(8,128)(2,1)} async-done(((bf16[1024,128]{1,0:T(8,128)(2,1)}), bf16[128,128]{1,0:T(8,128)(2,1)}) %reduce-scatter.69.cloned.1.call-update) | async-done | bytes 32784 | tf_op jit(solution)/shard_map/reduce_scatter | solution.py:327
  1859.7 30.4 %reduce-scatter.95.cloned.1.call-done = bf16[128,160]{1,0:T(8,128)(2,1)} async-done(((bf16[1024,160]{1,0:T(8,128)(2,1)}), bf16[128,160]{1,0:T(8,128)(2,1)}) %reduce-scatter.95.cloned.1.call-update) | async-done | bytes 40976
  1891.4 21.4 %all-reduce.12 = (f32[1,128]{1,0:T(1,128)}, f32[1,128]{1,0:T(1,128)}, f32[1,128]{1,0:T(1,128)}, f32[1,128]{1,0:T(1,128)}, f32[1,128]{1,0:T(1,128)}, /*index=5*/f...) all-reduce(f32[1,128]{1,0:T(1,128)S(1)} %add_bitcast_fusion.6, ...), channel_id=1, replica_groups=mesh['section'=2,'gx'=8,'gy'=8] {'gx'}, use_global_device_ids=true, to_apply=%region_78.79 | all-reduce | flops 1536 | bytes 12288 | tf_op jit(solution)/shard_map/psum | solution.py:340
  1912.8 18.9 all-reduce
  1931.9 33.3 %reduce-scatter.99.cloned.1.call-done = bf16[128,512]{1,0:T(8,128)(2,1)} async-done(((bf16[1024,512]{1,0:T(8,128)(2,1)}), bf16[128,512]{1,0:T(8,128)(2,1)}) %reduce-scatter.99.cloned.1.call-update) | async-done | bytes 131088
  1967.0 73.4 %reduce-scatter.71.cloned.1.call-done = bf16[128,512]{1,0:T(8,128)(2,1)} async-done(((bf16[1024,512]{1,0:T(8,128)(2,1)}), bf16[128,512]{1,0:T(8,128)(2,1)}) %reduce-scatter.71.cloned.1.call-update) | async-done | bytes 131088 | tf_op jit(solution)/shard_map/reduce_scatter | solution.py:333
  (670 shorter events, 383.7 us)
Async XLA Ops:
  8.0 118.2 %copy-start.148 = (f32[1,128]{1,0:T(1,128)S(1)}, f32[1,128]{1,0:T(1,128)}, u32[]{:S(2)}) copy-start(f32[1,128]{1,0:T(1,128)} %param.23) | copy-start | bytes 1540
  8.0 118.6 %copy-start.108 = (bf16[1,128,128]{2,1,0:T(8,128)(2,1)S(1)}, bf16[1,128,128]{2,1,0:T(8,128)(2,1)}, u32[]{:S(2)}) copy-start(bf16[1,128,128]{2,1,0:T(8,128)(2,1)} %param.24) | copy-start | bytes 98308
  8.1 268.3 %reduce-scatter.73.cloned.1.call-start = ((), (), s32[]{:S(2)}) async-start(), calls=%async_computation.36 | async-start | bytes 589824
  9.9 463.9 %copy-start.136 = (pred[640]{0:T(1024)(128)(4,1)}, pred[640]{0:T(1024)(128)(4,1)S(1)}, u32[]{:S(2)}) copy-start(pred[640]{0:T(1024)(128)(4,1)S(1)} %iota_compare_fusion) | copy-start | bytes 1924
  68.1 558.4 %copy-start = (bf16[1,1024,128]{2,1,0:T(8,128)(2,1)}, bf16[1,1024,128]{2,1,0:T(8,128)(2,1)S(1)}, u32[]{:S(2)}) copy-start(bf16[1,1024,128]{2,1,0:T(8,128)(2,1)S(1)} %all-gather) | copy-start | bytes 786436
  126.3 500.5 %copy-start.7 = (bf16[1,1024,128]{2,1,0:T(8,128)(2,1)}, bf16[1,1024,128]{2,1,0:T(8,128)(2,1)S(1)}, u32[]{:S(2)}) copy-start(bf16[1,1024,128]{2,1,0:T(8,128)(2,1)S(1)} %all-gather.1) | copy-start | bytes 786436
  155.1 473.1 %copy-start.2 = (bf16[1,1024,128]{2,1,0:T(8,128)(2,1)}, bf16[1,1024,128]{2,1,0:T(8,128)(2,1)S(1)}, u32[]{:S(2)}) copy-start(bf16[1,1024,128]{2,1,0:T(8,128)(2,1)S(1)} %all-gather.2) | copy-start | bytes 786436
  210.1 266.9 %copy-start.4 = (bf16[1,128,1024]{2,1,0:T(8,128)(2,1)}, bf16[1,128,1024]{2,1,0:T(8,128)(2,1)S(1)}, u32[]{:S(2)}) copy-start(bf16[1,128,1024]{2,1,0:T(8,128)(2,1)S(1)} %all-gather.3) | copy-start | bytes 786436
  213.7 92.0 %all-gather.9.cloned.1.call-start = ((), (), s32[]{:S(2)}) async-start(), calls=%async_computation.34 | async-start | bytes 1179648 | tf_op jit(solution)/shard_map/all_gather | solution.py:29
  214.2 131.3 %all-gather.11.cloned.1.call-start = ((), (), s32[]{:S(2)}) async-start(), calls=%async_computation.35 | async-start | bytes 1179648 | tf_op jit(solution)/shard_map/all_gather | solution.py:30
  214.8 165.2 %reduce-scatter.75.cloned.1.call-start = ((), (), s32[]{:S(2)}) async-start(), calls=%async_computation.37 | async-start | bytes 589824
  351.0 171.9 %reduce-scatter.77.cloned.1.call-start = ((), (), s32[]{:S(2)}) async-start(), calls=%async_computation.38 | async-start | bytes 589824
  381.2 4.3 collective-permute-start
  482.1 106.8 %reduce-scatter.79.cloned.1.call-start = ((), (), s32[]{:S(2)}) async-start(), calls=%async_computation.39 | async-start | bytes 589824
  560.4 178.1 %reduce-scatter.81.cloned.1.call-start = ((), (), s32[]{:S(2)}) async-start(), calls=%async_computation.40 | async-start | bytes 589824
  592.8 5.1 collective-permute-start.1
  697.9 113.4 %reduce-scatter.85.cloned.1.call-start = ((), (), s32[]{:S(2)}) async-start(), calls=%async_computation.42 | async-start | bytes 589824
  782.8 135.4 %reduce-scatter.53.cloned.1.call-start = ((), (), s32[]{:S(2)}) async-start(), calls=%async_computation.24 | async-start | bytes 368640 | tf_op jit(solution)/shard_map/reduce_scatter | solution.py:192
  856.6 128.3 %reduce-scatter.55.cloned.1.call-start = ((), (), s32[]{:S(2)}) async-start(), calls=%async_computation.25 | async-start | bytes 368640 | tf_op jit(solution)/shard_map/reduce_scatter | solution.py:198
  858.7 126.1 %copy-start.1 = (bf16[1,1024,128]{2,1,0:T(8,128)(2,1)S(1)}, bf16[1,1024,128]{2,1,0:T(8,128)(2,1)}, u32[]{:S(2)}) copy-start(bf16[1,1024,128]{2,1,0:T(8,128)(2,1)} %copy-done) | copy-start | bytes 786436
  860.7 160.2 %reduce-scatter.87.cloned.1.call-start = ((), (), s32[]{:S(2)}) async-start(), calls=%async_computation.43 | async-start | bytes 589824
  920.4 117.5 %copy-start.46 = (f32[2,80,128]{2,1,0:T(8,128)S(1)}, f32[2,80,128]{2,1,0:T(8,128)}, u32[]{:S(2)}) copy-start(f32[2,80,128]{2,1,0:T(8,128)} %copy-done.45) | copy-start | bytes 245764
  920.4 122.4 %copy-start.76 = (bf16[2,2,80,128]{3,2,1,0:T(8,128)(2,1)S(1)}, bf16[2,2,80,128]{3,2,1,0:T(8,128)(2,1)}, u32[]{:S(2)}) copy-start(bf16[2,2,80,128]{3,2,1,0:T(8,128)(2,1)} %param.35) | copy-start | bytes 245764
  920.4 122.4 %copy-start.131 = (f32[2,80]{1,0:T(2,128)S(1)}, f32[2,80]{1,0:T(2,128)}, u32[]{:S(2)}) copy-start(f32[2,80]{1,0:T(2,128)} %get-tuple-element.119) | copy-start | bytes 1924
  991.1 103.6 %reduce-scatter.89.cloned.1.call-start = ((), (), s32[]{:S(2)}) async-start(), calls=%async_computation.44 | async-start | bytes 589824
  1038.1 4.7 collective-permute-start.2
  1066.1 133.1 %reduce-scatter.57.cloned.1.call-start = ((), (), s32[]{:S(2)}) async-start(), calls=%async_computation.26 | async-start | bytes 368640 | tf_op jit(solution)/shard_map/reduce_scatter | solution.py:192
  1137.6 128.2 %reduce-scatter.59.cloned.1.call-start = ((), (), s32[]{:S(2)}) async-start(), calls=%async_computation.27 | async-start | bytes 368640 | tf_op jit(solution)/shard_map/reduce_scatter | solution.py:198
  1141.5 158.4 %reduce-scatter.91.cloned.1.call-start = ((), (), s32[]{:S(2)}) async-start(), calls=%async_computation.45 | async-start | bytes 589824
  1270.0 100.9 %reduce-scatter.93.cloned.1.call-start = ((), (), s32[]{:S(2)}) async-start(), calls=%async_computation.46 | async-start | bytes 589824
  1317.2 4.7 collective-permute-start.3
  1342.3 124.6 %reduce-scatter.61.cloned.1.call-start = ((), (), s32[]{:S(2)}) async-start(), calls=%async_computation.28 | async-start | bytes 368640 | tf_op jit(solution)/shard_map/reduce_scatter | solution.py:192
  1405.2 128.2 %reduce-scatter.63.cloned.1.call-start = ((), (), s32[]{:S(2)}) async-start(), calls=%async_computation.29 | async-start | bytes 368640 | tf_op jit(solution)/shard_map/reduce_scatter | solution.py:198
  1406.5 158.8 %reduce-scatter.83.cloned.1.call-start = ((), (), s32[]{:S(2)}) async-start(), calls=%async_computation.41 | async-start | bytes 589824
  1414.3 224.8 %reduce-scatter.97.cloned.1.call-start = ((), (), s32[]{:S(2)}) async-start(), calls=%async_computation.48 | async-start | bytes 294912
  1418.2 294.2 %reduce-scatter.65.cloned.1.call-start = ((), (), s32[]{:S(2)}) async-start(), calls=%async_computation.30 | async-start | bytes 294912 | tf_op jit(solution)/shard_map/reduce_scatter | solution.py:321
  1420.7 365.0 %reduce-scatter.67.cloned.1.call-start = ((), (), s32[]{:S(2)}) async-start(), calls=%async_computation.31 | async-start | bytes 294912 | tf_op jit(solution)/shard_map/reduce_scatter | solution.py:324
  1469.1 389.1 %reduce-scatter.69.cloned.1.call-start = ((), (), s32[]{:S(2)}) async-start(), calls=%async_computation.32 | async-start | bytes 294912 | tf_op jit(solution)/shard_map/reduce_scatter | solution.py:327
  1535.7 354.4 %reduce-scatter.95.cloned.1.call-start = ((), (), s32[]{:S(2)}) async-start(), calls=%async_computation.47 | async-start | bytes 589824
  1538.1 427.1 %reduce-scatter.99.cloned.1.call-start = ((), (), s32[]{:S(2)}) async-start(), calls=%async_computation.49 | async-start | bytes 1179648
  1543.0 497.4 %reduce-scatter.71.cloned.1.call-start = ((), (), s32[]{:S(2)}) async-start(), calls=%async_computation.33 | async-start | bytes 1179648 | tf_op jit(solution)/shard_map/reduce_scatter | solution.py:333
  1568.2 322.9 %copy-start.116 = (f32[2,80]{1,0:T(2,128)S(1)}, f32[2,80]{1,0:T(2,128)}, u32[]{:S(2)}) copy-start(f32[2,80]{1,0:T(2,128)} %copy-done.115) | copy-start | bytes 1924
  1568.2 322.9 %copy-start.118 = (f32[2,80]{1,0:T(2,128)S(1)}, f32[2,80]{1,0:T(2,128)}, u32[]{:S(2)}) copy-start(f32[2,80]{1,0:T(2,128)} %copy-done.117) | copy-start | bytes 1924
  1568.2 323.2 %copy-start.160 = (f32[128]{0:T(128)S(1)}, f32[128]{0:T(128)}, u32[]{:S(2)}) copy-start(f32[128]{0:T(128)} %get-tuple-element.35) | copy-start | bytes 1540
  1568.2 323.2 %copy-start.167 = (f32[128]{0:T(128)S(1)}, f32[128]{0:T(128)}, u32[]{:S(2)}) copy-start(f32[128]{0:T(128)} %get-tuple-element.33) | copy-start | bytes 1540
  1568.2 323.2 %copy-start.159 = (f32[128]{0:T(128)S(1)}, f32[128]{0:T(128)}, u32[]{:S(2)}) copy-start(f32[128]{0:T(128)} %get-tuple-element.53) | copy-start | bytes 1540
  1568.2 323.2 %copy-start.166 = (f32[128]{0:T(128)S(1)}, f32[128]{0:T(128)}, u32[]{:S(2)}) copy-start(f32[128]{0:T(128)} %get-tuple-element.52) | copy-start | bytes 1540
  1568.2 363.5 %copy-start.52 = (f32[2,80,128]{2,1,0:T(8,128)S(1)}, f32[2,80,128]{2,1,0:T(8,128)}, u32[]{:S(2)}) copy-start(f32[2,80,128]{2,1,0:T(8,128)} %copy-done.51) | copy-start | bytes 245764
  (166 other events, 4065.0 us)
Sparse Core Ops, SparseCore 0:
  213.8 62.4 reduce-scatter.72
  351.1 28.8 reduce-scatter.74
  482.2 40.7 reduce-scatter.76
  560.5 28.2 reduce-scatter.78
  698.0 40.4 reduce-scatter.80
  782.9 28.3 reduce-scatter.84
  991.2 29.6 reduce-scatter.86
  1066.2 28.3 reduce-scatter.88
  1270.2 29.6 reduce-scatter.90
  1342.5 28.4 reduce-scatter.92
Sparse Core Ops, SparseCore 1:
  216.7 79.6 all-gather.8
  298.7 46.8 all-gather.10
  856.7 61.5 reduce-scatter.52
  922.0 62.8 reduce-scatter.54
  1137.7 61.5 reduce-scatter.56
  1203.1 62.7 reduce-scatter.58
  1405.3 61.5 reduce-scatter.60
  1470.5 62.8 reduce-scatter.62
  1535.7 29.6 reduce-scatter.82
  1569.3 69.7 reduce-scatter.96
  1643.1 69.2 reduce-scatter.64
  1716.4 69.2 reduce-scatter.66
  1789.0 69.2 reduce-scatter.68
  1860.8 29.2 reduce-scatter.94
  1893.7 71.5 reduce-scatter.98
  1969.3 71.0 reduce-scatter.70
where the time goes:
time: 2060 us; the launch traced here: 2050 us
  waiting for transfers between devices  1150 us (56%)
  blocking collectives  658 us (32%)
  local copies, waits for them, and re-layouts  88.8 us (4%)
  matrix products  85.5 us (4%)
  other arithmetic  36.5 us (2%)
    unnamed x40, waiting for transfers between devices  471 us
    reduce_scatter x3, waiting for transfers between devices, backward_layer(): lax.psum_scatter(grad_value.reshape(value_rows.shape).astype(jnp.bfloat16...  193 us
    reduce_scatter x3, waiting for transfers between devices, backward_layer(): lax.psum_scatter(grad_key.reshape(key_rows.shape).astype(jnp.bfloat16), '...  153 us
    psum x6, blocking collectives, norm_backward(): first_sum, second_sum = lax.psum((first_sum, second_sum), 'gy')  96.3 us
    psum x6, blocking collectives, row_moments(): summed, square = lax.psum((summed, square), 'gy')  93.3 us
    all_gather x6, blocking collectives, gather_grad(): return lax.all_gather(values.astype(jnp.bfloat16), 'gy', axis=2, tiled=True)  88.2 us
    all_gather x3, blocking collectives, forward_layer(): lax.all_gather(value_part, 'gx', axis=1, tiled=True)  86.2 us
    all_gather x3, blocking collectives, forward_layer(): lax.all_gather(key_part, 'gx', axis=1, tiled=True)  85.6 us
  transfers between devices with their start and end apart: 30, of which 28 were waited for; matrix products, arithmetic and copies ran while one was open for 3% of the time, Pallas kernels for 0%

commit v1 on v0

v1 whole, which is shorter than its diff:
```python
import jax
import jax.numpy as jnp
from jax import lax
from jax.experimental import pallas as pl
from jax.experimental.pallas import tpu as pltpu
from jax.sharding import PartitionSpec as P

BF = jnp.bfloat16
F32 = jnp.float32
SEQ = 577
EPS = 1e-06
NEG = -1e30
ROWS = 160
TOK = 80
LANES = 128
WIDE = 1024
MESH = pl.DeviceIdType.MESH

K_X, K_O, K_M, K_D, K_G, K_N2, K_GM, K_N1 = range(8)
V_AG, V_AS, V_MG, V_MS, V_BQ, V_BV, V_BO, V_BD, V_BU = range(9)


def dot_nn(a, b):
    return lax.dot_general(a, b, (((1,), (0,)), ((), ())), preferred_element_type=F32)


def dot_nt(a, b):
    return lax.dot_general(a, b, (((1,), (1,)), ((), ())), preferred_element_type=F32)


def dot_tn(a, b):
    return lax.dot_general(a, b, (((0,), (0,)), ((), ())), preferred_element_type=F32)


def lanes(index):
    return pl.ds(pl.multiple_of(index * LANES, LANES), LANES)


def wait_bytes(ref, sem):
    pltpu.make_async_copy(ref, ref, sem).wait()


def put(src, dst, send_sem, recv_sem, device):
    pltpu.make_async_remote_copy(
        src_ref=src,
        dst_ref=dst,
        send_sem=send_sem,
        recv_sem=recv_sem,
        device_id=device,
        device_id_type=MESH,
    ).start()


def row_sum(values):
    return jnp.sum(values, axis=0, keepdims=True)


def three_parts(values):
    high = values.astype(BF).astype(F32)
    rest = values - high
    mid = rest.astype(BF).astype(F32)
    return high, mid, rest - mid


def kernel(
    images, counts, attn_gain, attn_shift, w_query, b_query, w_key, w_value, b_value, w_out,
    b_out, mlp_gain, mlp_shift, w_up, b_up, w_down, b_down, cotangent,
    act_o, ig_o, g_attn_gain, g_attn_shift, g_w_query, g_b_query, g_w_key, g_w_value, g_b_value,
    g_w_out, g_b_out, g_mlp_gain, g_mlp_shift, g_w_up, g_b_up, g_w_down, g_b_down,
    vec, cot, wqkv, wo, wup, wdn,
    xg, mg, gg, gmg, norm, unit, rstd, res, mid, gcur, gmid,
    stage, rsb, stat, kv, qg, dog, owna, attn_f, attn_b, aux, hid, pre,
    rest, ybuf, igbuf, s_dn, s_up, s_wo, s_qkv, s_vec, r_dn, r_up, r_wo, r_qkv, r_vec, vgrad,
    lsem, gy_send, gy_recv, st_send, st_recv, kv_send, kv_recv, do_send, do_recv,
    vec_send, vec_recv, w_send, w_recv, g_send, g_recv, a_send, a_recv, i_send, i_recv,
):
    s = lax.axis_index("section")
    gx = lax.axis_index("gx")
    gy = lax.axis_index("gy")
    other = 1 - s
    mine = lanes(gy)
    gx_lanes = lanes(gx)
    gx_rows = lanes(gx)

    barrier = pltpu.get_barrier_semaphore()

    def greet(device):
        pl.semaphore_signal(barrier, inc=1, device_id=device, device_id_type=MESH)

    gy_peers = [(s, gx, lax.rem(gy + k, 8)) for k in range(1, 8)]
    gx_peers = [(s, lax.rem(gx + k, 8), gy) for k in range(1, 8)]
    far_gx = [(other, lax.rem(gx + k, 8), gy) for k in range(8)]
    far_gy = [(other, gx, lax.rem(gy + k, 8)) for k in range(8)]
    for device in gy_peers + gx_peers + far_gx + far_gy[1:]:
        greet(device)

    own = [pltpu.make_async_copy(images.at[s], xg.at[0, :, mine], lsem.at[0])]
    own.append(pltpu.make_async_copy(cotangent.at[s], cot, lsem.at[1]))
    rows = [attn_gain, attn_shift, mlp_gain, mlp_shift, b_query, b_value, b_out, b_down]
    vec_own = []
    for row, ref in enumerate(rows):
        vec_own.append(pltpu.make_async_copy(ref, vec.at[s, row, :, mine], lsem.at[8 + row]))
    for part in range(4):
        vec_own.append(
            pltpu.make_async_copy(
                b_up.at[:, part * LANES : (part + 1) * LANES],
                vec.at[s, V_BU + part, :, mine],
                lsem.at[16 + part],
            )
        )
    w_own = []
    for part, ref in enumerate((w_query, w_key, w_value)):
        w_own.append(
            pltpu.make_async_copy(
                ref, wqkv.at[s, gx_rows, part * LANES : (part + 1) * LANES], lsem.at[2 + part]
            )
        )
    w_own.append(pltpu.make_async_copy(w_out, wo.at[s, :, gx_lanes], lsem.at[5]))
    w_own.append(pltpu.make_async_copy(w_up, wup.at[s, gx_rows, :], lsem.at[6]))
    w_own.append(pltpu.make_async_copy(w_down, wdn.at[s, :, gx_lanes], lsem.at[7]))
    for copy in own + vec_own + w_own:
        copy.start()

    pl.semaphore_wait(barrier, 29)

    for device in gy_peers:
        put(images.at[s], xg.at[0, :, mine], gy_send.at[K_X, 0], gy_recv.at[K_X, 0], device)
    for copy in vec_own:
        copy.wait()
    for near, group in ((0, gy_peers), (1, far_gy)):
        for device in group:
            block = vec.at[s, :, :, mine]
            put(block, block, vec_send.at[near], vec_recv.at[near], device)
    for copy in w_own:
        copy.wait()
    own[0].wait()
    own[1].wait()

    def w_block(group):
        if group == 0:
            return wqkv.at[s, gx_rows, :]
        if group == 1:
            return wo.at[s, :, gx_lanes]
        if group == 2:
            return wup.at[s, gx_rows, :]
        return wdn.at[s, :, gx_lanes]

    def send_weights(groups):
        for group in groups:
            block = w_block(group)
            for near, peers in ((0, gx_peers), (1, far_gx)):
                for device in peers:
                    put(block, block, w_send.at[group, near], w_recv.at[group, s], device)

    def wait_weights(group, l):
        if group == 0:
            seven, one = wqkv.at[l, 0:896, :], wqkv.at[l, 0:LANES, :]
        elif group == 1:
            seven, one = wo.at[l, :, 0:896], wo.at[l, :, 0:LANES]
        elif group == 2:
            seven, one = wup.at[l, 0:896, :], wup.at[l, 0:LANES, :]
        else:
            seven, one = wdn.at[l, :, 0:896], wdn.at[l, :, 0:LANES]
        whole = (wqkv, wo, wup, wdn)[group].at[l]

        @pl.when(l == s)
        def _():
            wait_bytes(seven, w_recv.at[group, l])

        @pl.when(l != s)
        def _():
            wait_bytes(whole, w_recv.at[group, l])

    @pl.when(s == 0)
    def _():
        send_weights((0, 1, 2, 3))

    def gather_gy(buffer, kind, l):
        block = buffer.at[l, :, mine]
        for device in gy_peers:
            put(block, block, gy_send.at[kind, l], gy_recv.at[kind, l], device)

    def wait_gather(buffer, kind, l):
        wait_bytes(buffer.at[l, :, 0:896], gy_recv.at[kind, l])

    slot_of = {K_O: 0, K_D: 1, K_N2: 2, K_N1: 3}

    def scatter_gy(partial, kind, l):
        slot = slot_of[kind]
        stage[slot, l] = partial.astype(BF)
        for _, _, peer in gy_peers:
            put(
                stage.at[slot, l, :, lanes(peer)],
                rsb.at[slot, l, gy],
                gy_send.at[kind, l],
                gy_recv.at[kind, l],
                (s, gx, peer),
            )
        rsb[slot, l, gy] = stage[slot, l, :, mine]

    def wait_scatter(kind, l):
        slot = slot_of[kind]
        wait_bytes(rsb.at[slot, l, 0:7], gy_recv.at[kind, l])
        total = rsb[slot, l, 0].astype(F32)
        for source in range(1, 8):
            total = total + rsb[slot, l, source].astype(F32)
        return total

    lane_id = lax.broadcasted_iota(jnp.int32, (TOK, LANES), 1)
    low_half = lane_id < 64
    head_mask = [low_half.astype(F32).astype(BF), (lane_id >= 64).astype(F32).astype(BF)]

    def two_heads(block):
        return jnp.concatenate([block * head_mask[0], block * head_mask[1]], axis=0)

    def join_heads(both):
        return jnp.where(low_half, both[:TOK], both[TOK:])

    def masked_lanes(low, count, value, height):
        ids = lax.broadcasted_iota(jnp.int32, (height, LANES), 1)
        return jnp.where((ids >= low) & (ids < low + count), value, 0.0).astype(BF)

    key_ok = lax.broadcasted_iota(jnp.int32, (ROWS, 640), 1) < SEQ

    def norm_rows(values, gain_row, shift_row, which, l):
        center = values - jnp.mean(values, axis=-1, keepdims=True)
        spread = jnp.mean(center * center, axis=-1, keepdims=True)
        scale = lax.rsqrt(spread + EPS)
        xhat = center * scale
        unit[which, l] = xhat
        rstd[which, l] = jnp.broadcast_to(scale, (ROWS, LANES))
        norm[which, l] = (xhat * vec[l, gain_row] + vec[l, shift_row]).astype(BF)

    res[...] = xg[0, :, mine].astype(F32)
    wait_bytes(vec.at[s, :, :, 0:896], vec_recv.at[0])
    wait_bytes(vec.at[other], vec_recv.at[1])

    def forward(l, carry):
        wait_gather(xg, K_X, l)
        norm_rows(xg[l].astype(F32), V_AG, V_AS, 0, l)
        wait_weights(0, l)
        qkv = dot_nn(norm[0, l], wqkv[l])
        key = qkv[:, LANES : 2 * LANES].astype(BF)
        value = (qkv[:, 2 * LANES :] + vec[l, V_BV, :, mine]).astype(BF)
        query = (qkv[:, :LANES] + vec[l, V_BQ, :, mine]).astype(BF) * jnp.asarray(0.125, BF)
        for c in range(2):
            kv[l, 0, c, gx] = key[c * TOK : (c + 1) * TOK]
            kv[l, 1, c, gx] = value[c * TOK : (c + 1) * TOK]
            qg[l, c, gx] = query[c * TOK : (c + 1) * TOK]
        for device in gx_peers:
            block = kv.at[l, :, :, gx]
            put(block, block, kv_send.at[0, l], kv_recv.at[0, l], device)
        for device in gx_peers:
            block = qg.at[l, :, gx]
            put(block, block, kv_send.at[1, l], kv_recv.at[1, l], device)

        @pl.when((s == 1) & (l == 0))
        def _():
            send_weights((0, 1, 2, 3))

        wait_bytes(kv.at[l, :, :, 0:7], kv_recv.at[0, l])
        for c in range(2):
            all_keys = kv[l, 0, c].reshape(640, LANES)
            all_values = kv[l, 1, c].reshape(640, LANES)
            scores = dot_nt(two_heads(qg[l, c, gx]), all_keys)
            scores = jnp.where(key_ok, scores, NEG)
            highest = jnp.max(scores, axis=-1, keepdims=True)
            exponent = jnp.exp(scores - highest)
            summed = jnp.sum(exponent, axis=-1, keepdims=True)
            full = exponent / summed
            weights = full.astype(BF)
            rest[c] = (full - weights.astype(F32)).astype(BF)
            mixed = join_heads(dot_nn(weights, all_values))
            attn_f[l, c * TOK : (c + 1) * TOK] = mixed
            attn_b[l, c * TOK : (c + 1) * TOK] = mixed.astype(BF)
            logs = highest + jnp.log(summed)
            line = jnp.zeros((TOK, LANES), F32)
            for head in range(2):
                for at, part in enumerate(three_parts(logs[head * TOK : (head + 1) * TOK])):
                    line = jnp.where(lane_id == head * 3 + at, part, line)
            aux[l, c * TOK : (c + 1) * TOK] = line
        wait_weights(1, l)
        scatter_gy(dot_nn(attn_b[l], wo[l]), K_O, l)
        for c in range(2):
            all_values = kv[l, 1, c].reshape(640, LANES)
            attn_f[l, c * TOK : (c + 1) * TOK] += join_heads(dot_nn(rest[c], all_values))
        middle = res[...] + wait_scatter(K_O, l) + vec[l, V_BO, :, mine]
        mid[...] = middle
        mg[l, :, mine] = middle.astype(BF)
        gather_gy(mg, K_M, l)
        wait_gather(mg, K_M, l)
        norm_rows(mg[l].astype(F32), V_MG, V_MS, 1, l)
        wait_weights(2, l)
        bias = jnp.concatenate([vec[l, V_BU + part, :, mine] for part in range(4)], axis=1)
        pre_act = dot_nn(norm[1, l], wup[l]) + bias
        gate = 0.5 * (1.0 + lax.erf(pre_act * 0.7071067811865476))
        hid[l] = (pre_act * gate).astype(BF)
        wait_weights(3, l)
        scatter_gy(dot_nn(hid[l], wdn[l]), K_D, l)
        pre[l] = gate + pre_act * jnp.exp(-0.5 * pre_act * pre_act) * 0.3989422804014327
        output = (mid[...] + wait_scatter(K_D, l) + vec[l, V_BD, :, mine]).astype(BF)
        ybuf[l] = output
        res[...] = output.astype(F32)

        @pl.when(l == 0)
        def _():
            xg[1, :, mine] = output
            gather_gy(xg, K_X, 1)

        @pl.when(l == s)
        def _():
            pltpu.make_async_copy(ybuf.at[l], act_o.at[s], a_recv.at[0]).start()

        @pl.when(l != s)
        def _():
            put(ybuf.at[l], act_o.at[s], a_send.at[0], a_recv.at[0], (other, gx, gy))

        return carry

    lax.fori_loop(0, 2, forward, 0)

    row_id = lax.broadcasted_iota(jnp.int32, (ROWS, LANES), 0)
    image_id = (row_id >= TOK).astype(jnp.int32)
    position = row_id - image_id * TOK + gx * TOK
    live = ((image_id < counts[s]) & (position < SEQ)).astype(F32)
    gcur[...] = cot[...].astype(F32) * live

    def send_grads(groups, l):
        for group in groups:
            for j in range(8):
                k = lax.rem(gx + j, 8)
                if group == 0:
                    src = s_qkv.at[l, lanes(k), :]
                elif group == 1:
                    src = s_wo.at[l, :, lanes(k)]
                elif group == 2:
                    src = s_up.at[l, lanes(k), :]
                elif group == 3:
                    src = s_dn.at[l, :, lanes(k)]
                else:
                    src = s_vec.at[l]
                dst = (r_qkv, r_wo, r_up, r_dn, r_vec)[group].at[s * 8 + gx]
                if j == 0:

                    @pl.when(l == s)
                    def _(src=src, dst=dst, group=group):
                        pltpu.make_async_copy(src, dst, g_recv.at[group]).start()

                    @pl.when(l != s)
                    def _(src=src, dst=dst, group=group, k=k):
                        put(src, dst, g_send.at[group, l], g_recv.at[group], (l, k, gy))

                else:
                    put(src, dst, g_send.at[group, l], g_recv.at[group], (l, k, gy))

    def send_stats(first, second, which, l):
        ids = lax.broadcasted_iota(jnp.int32, (ROWS, LANES), 1)
        both = jnp.where(ids == 0, first, jnp.where(ids == 1, second, 0.0))
        both = jnp.concatenate([both, jnp.zeros((256 - ROWS, LANES), F32)], axis=0)
        stat[which, l, gy] = both.T[:8]
        for device in gy_peers:
            block = stat.at[which, l, gy]
            put(block, block, st_send.at[which, l], st_recv.at[which, l], device)

    def wait_stats(which, l):
        wait_bytes(stat.at[which, l, 0:7], st_recv.at[which, l])
        total = stat[which, l, 0]
        for source in range(1, 8):
            total = total + stat[which, l, source]
        total = jnp.concatenate([total, jnp.zeros((LANES - 8, 256), F32)], axis=0).T
        return total[:ROWS, 0:1], total[:ROWS, 1:2]

    def norm_back_send(partial, which, gain_row, kind, l):
        scatter_gy(partial, kind, l)
        weighted = partial * vec[l, gain_row]
        first = jnp.sum(weighted, axis=-1, keepdims=True)
        second = jnp.sum(weighted * unit[which, l], axis=-1, keepdims=True)
        send_stats(first, second, which, l)

    def norm_back_take(which, gain_row, kind, l, gain_slot, shift_slot):
        grad = wait_scatter(kind, l)
        first, second = wait_stats(which, l)
        xhat = unit[which, l, :, mine]
        vgrad[gain_slot] = row_sum(grad * xhat)
        vgrad[shift_slot] = row_sum(grad)
        inner = grad * vec[l, gain_row, :, mine]
        return rstd[which, l] * (
            inner - first * (1.0 / WIDE) - xhat * (second * (1.0 / WIDE))
        )

    def backward(step, carry):
        l = 1 - step
        grad_out = gcur[...]
        gg[l, :, mine] = grad_out.astype(BF)
        gather_gy(gg, K_G, l)
        vgrad[V_BD] = row_sum(grad_out)
        wait_gather(gg, K_G, l)
        grad_hid = dot_nt(gg[l], wdn[l])
        grad_pre32 = grad_hid * pre[l]
        grad_pre = grad_pre32.astype(BF)
        norm_back_send(dot_nt(grad_pre, wup[l]), 1, V_MG, K_N2, l)
        up_sum = row_sum(grad_pre.astype(F32))
        for part in range(4):
            vgrad[V_BU + part] = up_sum[:, part * LANES : (part + 1) * LANES]
        s_dn[l] = dot_tn(hid[l], gg[l]).astype(BF)
        send_grads((3,), l)
        s_up[l] = dot_tn(norm[1, l], grad_pre).astype(BF)
        send_grads((2,), l)
        grad_mid = gcur[...] + norm_back_take(1, V_MG, K_N2, l, V_MG, V_MS)
        gmid[...] = grad_mid
        gmg[l, :, mine] = grad_mid.astype(BF)
        gather_gy(gmg, K_GM, l)
        vgrad[V_BO] = row_sum(grad_mid)
        wait_gather(gmg, K_GM, l)
        grad_mixed = dot_nt(gmg[l], wo[l]).astype(BF)
        grad_mixed32 = grad_mixed.astype(F32)
        for c in range(2):
            part32 = grad_mixed32[c * TOK : (c + 1) * TOK]
            product = part32 * attn_f[l, c * TOK : (c + 1) * TOK]
            line = aux[l, c * TOK : (c + 1) * TOK]
            for head in range(2):
                picked = jnp.where(low_half == (head == 0), product, 0.0)
                delta = jnp.sum(picked, axis=-1, keepdims=True)
                for at, part in enumerate(three_parts(delta)):
                    line = jnp.where(lane_id == 6 + head * 3 + at, part, line)
            dog[l, c, gx, :, 0:LANES] = grad_mixed[c * TOK : (c + 1) * TOK]
            dog[l, c, gx, :, LANES:] = line.astype(BF)
        for device in gx_peers:
            block = dog.at[l, :, gx]
            put(block, block, do_send.at[l], do_recv.at[l], device)
        s_wo[l] = dot_tn(attn_b[l], gmg[l]).astype(BF)
        send_grads((1,), l)

        @pl.when(l == 1)
        def _():
            wait_bytes(qg.at[0, :, 0:7], kv_recv.at[1, 0])
            wait_bytes(qg.at[1, :, 0:7], kv_recv.at[1, 1])

        wait_bytes(dog.at[l, :, 0:7], do_recv.at[l])
        key_side = masked_lanes(0, 6, -1.0, 640)
        value_side = masked_lanes(6, 6, -1.0, 640)
        row_ids = lax.broadcasted_iota(jnp.int32, (ROWS, 640), 0)
        key_pos = jnp.where(row_ids >= TOK, row_ids - TOK, row_ids) + gx * TOK
        own_ok = key_pos < SEQ
        for c in range(2):
            all_keys = kv[l, 0, c].reshape(640, LANES)
            all_values = kv[l, 1, c].reshape(640, LANES)
            all_query = qg[l, c].reshape(640, LANES)
            all_grads = dog[l, c].reshape(640, 2 * LANES)
            all_aux = all_grads[:, LANES:]
            all_mixed = all_grads[:, :LANES]
            my_aux = dog[l, c, gx, :, LANES:]
            my_log = jnp.concatenate(
                [my_aux * masked_lanes(0, 3, 1.0, TOK), my_aux * masked_lanes(3, 3, 1.0, TOK)],
                axis=0,
            )
            my_delta = jnp.concatenate(
                [my_aux * masked_lanes(6, 3, 1.0, TOK), my_aux * masked_lanes(9, 3, 1.0, TOK)],
                axis=0,
            )
            my_query = jnp.concatenate([two_heads(qg[l, c, gx]), my_log], axis=1)
            my_mixed = jnp.concatenate([two_heads(dog[l, c, gx, :, 0:LANES]), my_delta], axis=1)
            scores = dot_nt(my_query, jnp.concatenate([all_keys, key_side], axis=1))
            weights = jnp.exp(jnp.where(key_ok, scores, NEG))
            inner = dot_nt(my_mixed, jnp.concatenate([all_values, value_side], axis=1))
            grad_scores = (weights * inner).astype(BF)
            grad_query = join_heads(dot_nn(grad_scores, all_keys)) * 0.125
            owna[c * TOK : (c + 1) * TOK, 0:LANES] = grad_query.astype(BF)

            key_log = jnp.concatenate(
                [masked_lanes(0, 3, -1.0, TOK), masked_lanes(3, 3, -1.0, TOK)], axis=0
            )
            key_delta = jnp.concatenate(
                [masked_lanes(6, 3, -1.0, TOK), masked_lanes(9, 3, -1.0, TOK)], axis=0
            )
            my_key = jnp.concatenate([two_heads(kv[l, 0, c, gx]), key_log], axis=1)
            my_value = jnp.concatenate([two_heads(kv[l, 1, c, gx]), key_delta], axis=1)
            scores = dot_nt(my_key, jnp.concatenate([all_query, all_aux], axis=1))
            weights = jnp.exp(jnp.where(own_ok, scores, NEG))
            inner = dot_nt(my_value, all_grads)
            grad_scores = (weights * inner).astype(BF)
            grad_key = join_heads(dot_nn(grad_scores, all_query))
            grad_value = join_heads(dot_nn(weights.astype(BF), all_mixed))
            owna[c * TOK : (c + 1) * TOK, LANES : 2 * LANES] = grad_key.astype(BF)
            owna[c * TOK : (c + 1) * TOK, 2 * LANES :] = grad_value.astype(BF)
        grad_qkv = owna[...]
        norm_back_send(dot_nt(grad_qkv, wqkv[l]), 0, V_AG, K_N1, l)
        s_qkv[l] = dot_tn(norm[0, l], grad_qkv).astype(BF)
        send_grads((0,), l)
        bias_sum = row_sum(grad_qkv.astype(F32))
        vgrad[V_BQ] = bias_sum[:, :LANES]
        vgrad[V_BV] = bias_sum[:, 2 * LANES :]
        grad_in = gmid[...] + norm_back_take(0, V_AG, K_N1, l, V_AG, V_AS)
        igbuf[l] = grad_in
        gcur[...] = grad_in.astype(BF).astype(F32)
        s_vec[l] = vgrad[...]
        send_grads((4,), l)

        @pl.when(l == s)
        def _():
            pltpu.make_async_copy(igbuf.at[l], ig_o.at[s], i_recv.at[0]).start()

        @pl.when(l != s)
        def _():
            put(igbuf.at[l], ig_o.at[s], i_send.at[0], i_recv.at[0], (other, gx, gy))

        return carry

    lax.fori_loop(0, 2, backward, 0)

    def sum_of(ref):
        total = ref[0].astype(F32)
        for source in range(1, 16):
            total = total + ref[source].astype(F32)
        return total

    wait_bytes(r_dn, g_recv.at[3])
    g_w_down[...] = sum_of(r_dn)
    wait_bytes(r_up, g_recv.at[2])
    g_w_up[...] = sum_of(r_up)
    wait_bytes(r_wo, g_recv.at[1])
    g_w_out[...] = sum_of(r_wo)
    wait_bytes(r_qkv, g_recv.at[0])
    total = sum_of(r_qkv)
    g_w_query[...] = total[:, :LANES]
    g_w_key[...] = total[:, LANES : 2 * LANES]
    g_w_value[...] = total[:, 2 * LANES :]
    wait_bytes(r_vec, g_recv.at[4])
    total = sum_of(r_vec)
    g_attn_gain[...] = total[V_AG]
    g_attn_shift[...] = total[V_AS]
    g_mlp_gain[...] = total[V_MG]
    g_mlp_shift[...] = total[V_MS]
    g_b_query[...] = total[V_BQ]
    g_b_value[...] = total[V_BV]
    g_b_out[...] = total[V_BO]
    g_b_down[...] = total[V_BD]
    for part in range(4):
        g_b_up[:, part * LANES : (part + 1) * LANES] = total[V_BU + part]
    wait_bytes(act_o, a_recv.at[0])
    wait_bytes(ig_o, i_recv.at[0])

    wait_bytes(ybuf.at[0], a_send.at[0])
    wait_bytes(igbuf.at[0], i_send.at[0])
    wait_bytes(vec.at[s, :, :, 0:896], vec_send.at[0])
    wait_bytes(vec.at[s], vec_send.at[1])
    wholes = (wqkv, wo, wup, wdn)
    sevens = (
        wqkv.at[0, 0:896, :],
        wo.at[0, :, 0:896],
        wup.at[0, 0:896, :],
        wdn.at[0, :, 0:896],
    )
    for group in range(4):
        wait_bytes(sevens[group], w_send.at[group, 0])
        wait_bytes(wholes[group].at[0], w_send.at[group, 1])
    received = (r_qkv, r_wo, r_up, r_dn, r_vec)
    for l in range(2):
        for kind, buffer in ((K_X, xg), (K_M, mg), (K_G, gg), (K_GM, gmg)):
            wait_bytes(buffer.at[l, :, 0:896], gy_send.at[kind, l])
        for kind, slot in slot_of.items():
            wait_bytes(rsb.at[slot, l, 0:7], gy_send.at[kind, l])
        for which in range(2):
            wait_bytes(stat.at[which, l, 0:7], st_send.at[which, l])
        wait_bytes(kv.at[l, :, :, 0:7], kv_send.at[0, l])
        wait_bytes(qg.at[l, :, 0:7], kv_send.at[1, l])
        wait_bytes(dog.at[l, :, 0:7], do_send.at[l])

        @pl.when(s == l)
        def _(l=l):
            for group in range(5):
                wait_bytes(received[group].at[0:7], g_send.at[group, l])

        @pl.when(s != l)
        def _(l=l):
            for group in range(5):
                wait_bytes(received[group].at[0:8], g_send.at[group, l])


def local(
    images, counts, attn_gain, attn_shift, w_query, b_query, w_key, w_value, b_value, w_out,
    b_out, mlp_gain, mlp_shift, w_up, b_up, w_down, b_down, cotangent,
):
    anywhere = pl.BlockSpec(memory_space=pl.ANY)
    in_vmem = pl.BlockSpec(memory_space=pltpu.VMEM)
    in_smem = pl.BlockSpec(memory_space=pltpu.SMEM)
    in_specs = [anywhere, in_smem] + [anywhere] * 16
    row = jax.ShapeDtypeStruct((1, LANES), F32)
    square = jax.ShapeDtypeStruct((LANES, LANES), F32)
    out_shape = [
        jax.ShapeDtypeStruct((2, ROWS, LANES), BF),
        jax.ShapeDtypeStruct((2, ROWS, LANES), F32),
        row, row, square, row, square, square, row, square, row, row, row,
        jax.ShapeDtypeStruct((LANES, 512), F32),
        jax.ShapeDtypeStruct((1, 512), F32),
        jax.ShapeDtypeStruct((512, LANES), F32),
        row,
    ]
    vmem = pltpu.VMEM
    scratch = [
        vmem((2, 12, 1, WIDE), F32),
        vmem((ROWS, LANES), BF),
        vmem((2, WIDE, 384), BF),
        vmem((2, LANES, WIDE), BF),
        vmem((2, WIDE, 512), BF),
        vmem((2, 512, WIDE), BF),
        vmem((2, ROWS, WIDE), BF),
        vmem((2, ROWS, WIDE), BF),
        vmem((2, ROWS, WIDE), BF),
        vmem((2, ROWS, WIDE), BF),
        vmem((2, 2, ROWS, WIDE), BF),
        vmem((2, 2, ROWS, WIDE), F32),
        vmem((2, 2, ROWS, LANES), F32),
        vmem((ROWS, LANES), F32),
        vmem((ROWS, LANES), F32),
        vmem((ROWS, LANES), F32),
        vmem((ROWS, LANES), F32),
        vmem((4, 2, ROWS, WIDE), BF),
        vmem((4, 2, 8, ROWS, LANES), BF),
        vmem((2, 2, 8, 8, 256), F32),
        vmem((2, 2, 2, 8, TOK, LANES), BF),
        vmem((2, 2, 8, TOK, LANES), BF),
        vmem((2, 2, 8, TOK, 2 * LANES), BF),
        vmem((ROWS, 384), BF),
        vmem((2, ROWS, LANES), F32),
        vmem((2, ROWS, LANES), BF),
        vmem((2, ROWS, LANES), F32),
        vmem((2, ROWS, 512), BF),
        vmem((2, ROWS, 512), F32),
        vmem((2, ROWS, 640), BF),
        vmem((2, ROWS, LANES), BF),
        vmem((2, ROWS, LANES), F32),
        vmem((2, 512, WIDE), BF),
        vmem((2, WIDE, 512), BF),
        vmem((2, LANES, WIDE), BF),
        vmem((2, WIDE, 384), BF),
        vmem((2, 12, 1, LANES), F32),
        vmem((16, 512, LANES), BF),
        vmem((16, LANES, 512), BF),
        vmem((16, LANES, LANES), BF),
        vmem((16, LANES, 384), BF),
        vmem((16, 12, 1, LANES), F32),
        vmem((12, 1, LANES), F32),
        pltpu.SemaphoreType.DMA((20,)),
        pltpu.SemaphoreType.DMA((8, 2)),
        pltpu.SemaphoreType.DMA((8, 2)),
        pltpu.SemaphoreType.DMA((2, 2)),
        pltpu.SemaphoreType.DMA((2, 2)),
        pltpu.SemaphoreType.DMA((2, 2)),
        pltpu.SemaphoreType.DMA((2, 2)),
        pltpu.SemaphoreType.DMA((2,)),
        pltpu.SemaphoreType.DMA((2,)),
        pltpu.SemaphoreType.DMA((2,)),
        pltpu.SemaphoreType.DMA((2,)),
        pltpu.SemaphoreType.DMA((4, 2)),
        pltpu.SemaphoreType.DMA((4, 2)),
        pltpu.SemaphoreType.DMA((5, 2)),
        pltpu.SemaphoreType.DMA((5,)),
        pltpu.SemaphoreType.DMA((1,)),
        pltpu.SemaphoreType.DMA((1,)),
        pltpu.SemaphoreType.DMA((1,)),
        pltpu.SemaphoreType.DMA((1,)),
    ]
    outs = pl.pallas_call(
        kernel,
        out_shape=out_shape,
        in_specs=in_specs,
        out_specs=[in_vmem] * 17,
        scratch_shapes=scratch,
        compiler_params=pltpu.CompilerParams(
            collective_id=0, has_side_effects=True, vmem_limit_bytes=58 * 1024 * 1024
        ),
        cost_estimate=pl.CostEstimate(
            flops=4_000_000_000, bytes_accessed=8_000_000, transcendentals=4_000_000
        ),
        name="two_sections",
    )(
        images.reshape(2, ROWS, LANES), counts, attn_gain, attn_shift, w_query[0], b_query,
        w_key[0], w_value[0], b_value, w_out[0], b_out, mlp_gain, mlp_shift, w_up[0], b_up,
        w_down[0], b_down, cotangent.reshape(2, ROWS, LANES),
    )
    outs = list(outs)
    shape = (1,) + images.shape
    outs[0] = outs[0].reshape(shape)
    outs[1] = outs[1].reshape(shape)
    for index in (4, 6, 7, 9, 13, 15):
        outs[index] = outs[index][None]
    return tuple(outs)


def solution(mesh):
    vector = P("section", "gy")
    in_block = P("section", "gx", "gy")
    out_block = P("section", "gy", "gx")
    rows = P(None, None, "gx", "gy")
    in_specs = (
        rows, P(), vector, vector, in_block, vector, in_block, in_block, vector, out_block,
        vector, vector, vector, in_block, vector, out_block, vector, rows,
    )
    results = P("section", None, None, "gx", "gy")
    out_specs = (
        results, results, vector, vector, in_block, vector, in_block, in_block, vector,
        out_block, vector, vector, vector, in_block, vector, out_block, vector,
    )
    return jax.shard_map(local, mesh=mesh, in_specs=in_specs, out_specs=out_specs, check_vma=False)
```

time: 2060 us -> 320 us (0.16)
  waiting for transfers between devices: 1150 us -> 0 us
  blocking collectives: 658 us -> 0 us
  Pallas kernels: 0 us -> 308 us
  matrix products: 85.5 us -> 0 us
  local copies, waits for them, and re-layouts: 88.8 us -> 11.3 us
  other arithmetic: 36.5 us -> 0 us
    reduce_scatter x10 -> x0, waiting for transfers between devices: 635 us -> none  [the longest x3 193 us: backward_layer(): lax.psum_scatter(grad_value.reshape(value_rows.shape).astype(jnp.bfloat16...]
    unnamed x40 -> x0, waiting for transfers between devices: 471 us -> none
    all_gather x22 -> x0, blocking collectives: 447 us -> none  [the longest x6 88.2 us: gather_grad(): return lax.all_gather(values.astype(jnp.bfloat16), 'gy', axis=2, tiled=True)]
    pallas_call x0 -> x1, Pallas kernels: none -> 308 us  [local(): pl.pallas_call(kernel, out_shape=out_shape, in_specs=in_specs, out_specs=...]
    psum x13 -> x0, blocking collectives: 211 us -> none  [the longest x6 96.3 us: norm_backward(): first_sum, second_sum = lax.psum((first_sum, second_sum), 'gy')]
    dot_general x72 -> x0, matrix products: 85.5 us -> none  [contract(): jnp.einsum(pattern, left_side, right_side, preferred_element_type=jnp.flo...]
    unnamed x422 -> x49, local copies, waits for them, and re-layouts: 69.9 us -> 11.3 us
    all_gather x2 -> x0, waiting for transfers between devices: 38.1 us -> none  [the longest x1 38.1 us: fetch_blocks(): lax.all_gather(own_blocks[5], 'gx', axis=1, tiled=True)]
  transfers between devices with their start and end apart: 30 -> 0, of which waited for: 28 -> 0; matrix products, arithmetic and copies ran while one was open for 3% -> 0% of each run, Pallas kernels for 0% -> 0%
where the time goes in v1:
time: 320 us
  Pallas kernels  308 us (96%)
  local copies, waits for them, and re-layouts  11.3 us (4%)
    pallas_call x1, Pallas kernels, local(): pl.pallas_call(kernel, out_shape=out_shape, in_specs=in_specs, out_specs=...  308 us
    unnamed x49, local copies, waits for them, and re-layouts  11.3 us

profile of v1, /device:TPU:1, one launch (start us, length us, event | category | flops | bytes accessed | tf_op | source)
XLA Modules:
  0.0 319.6 jit_solution(16869011970915844970)
XLA Ops:
  0.7 307.6 %two_sections.1 = (bf16[2,160,128]{2,1,0:T(8,128)(2,1)}, f32[2,160,128]{2,1,0:T(8,128)}, f32[1,128]{1,0:T(1,128)}, f32[1,128]{1,0:T(1,128)}, f32[128,128]{1,0:T(...) custom-call(bf16[2,160,128]{2,1,0:T(8,128)(2,1)} %bitcast.26, ...), custom_call_target="tpu_custom_call" | custom-call | flops 4000000000 | bytes 8000000 | tf_op jit(solution)/shard_map/two_sections/pallas_call | solution.py:664
  308.3 0.0 copy-start.2
  308.3 1.6 copy.52
  309.9 0.0 copy-done.2
  309.9 0.0 copy-start.15
  309.9 0.0 copy-start.6
  309.9 0.0 copy-start.13
  309.9 0.0 copy-start.5
  309.9 0.0 copy-start.4
  309.9 0.7 copy.53
  310.6 0.0 copy-done.15
  310.6 0.5 copy.54
  311.1 0.2 copy-done.14
  311.2 0.5 copy.55
  311.8 0.0 copy-done.6
  311.8 0.6 copy.56
  312.4 0.0 copy-done.13
  312.4 0.5 copy.57
  312.9 0.0 copy-done.5
  312.9 0.6 copy.58
  313.5 0.0 copy-done.4
  313.5 0.0 copy-start.12
  313.5 0.0 copy-start.3
  313.5 0.6 copy.59
  314.2 0.0 copy-done.12
  314.2 0.5 copy.60
  314.7 0.0 copy-done.3
  314.7 0.0 copy-start.11
  314.7 0.6 copy.61
  315.3 0.0 copy-done.11
  315.4 0.0 copy-start.10
  315.4 0.5 copy.62
  315.9 0.1 copy-done.10
  315.9 0.0 copy-start.9
  315.9 0.5 copy.63
  316.4 0.1 copy-done.9
  316.6 0.5 copy.64
  317.1 0.0 copy-done.1
  317.1 0.0 copy-start.7
  317.1 0.0 copy-start
  317.1 0.7 copy.65
  317.8 0.0 copy-done.7
  317.8 0.6 copy.66
  318.4 0.0 copy-done
  318.4 0.0 copy-start.8
  318.4 0.7 copy.67
  319.1 0.0 copy-done.8
  319.1 0.5 copy.68
  (2 shorter events, 0.0 us)
Async XLA Ops:
  308.3 1.6 copy-start.2
  309.9 0.7 copy-start.15
  309.9 1.9 copy-start.6
  309.9 2.5 copy-start.13
  309.9 3.0 copy-start.5
  309.9 3.6 %copy-start.4 = (f32[128,128]{1,0:T(8,128)S(1)}, f32[128,128]{1,0:T(8,128)}, u32[]{:S(2)}) copy-start(f32[128,128]{1,0:T(8,128)} %get-tuple-element.41) | copy-start | bytes 196612
  310.6 0.7 copy-start.14
  311.8 5.3 %copy-start.1 = (f32[128,512]{1,0:T(8,128)S(1)}, f32[128,512]{1,0:T(8,128)}, u32[]{:S(2)}) copy-start(f32[128,512]{1,0:T(8,128)} %get-tuple-element.47) | copy-start | bytes 786436
  313.5 0.6 copy-start.12
  313.5 1.1 copy-start.3
  314.7 0.7 copy-start.11
  315.4 0.6 copy-start.10
  315.9 0.7 copy-start.9
  317.1 0.7 copy-start.7
  317.1 1.3 copy-start
  318.4 0.7 copy-start.8

commit v2 on v1

v2 whole, which is shorter than its diff:
```python
import jax
import jax.numpy as jnp
from jax import lax
from jax.experimental import pallas as pl
from jax.experimental.pallas import tpu as pltpu
from jax.sharding import PartitionSpec as P

BF = jnp.bfloat16
F32 = jnp.float32
SEQ = 577
EPS = 1e-06
NEG = -1e30
ROWS = 160
TOK = 80
LANES = 128
WIDE = 1024
MESH = pl.DeviceIdType.MESH

K_X, K_O, K_M, K_D, K_G, K_N2, K_GM, K_N1 = range(8)
V_AG, V_AS, V_MG, V_MS, V_BQ, V_BV, V_BO, V_BD, V_BU = range(9)


def dot_nn(a, b):
    return lax.dot_general(a, b, (((1,), (0,)), ((), ())), preferred_element_type=F32)


def dot_nt(a, b):
    return lax.dot_general(a, b, (((1,), (1,)), ((), ())), preferred_element_type=F32)


def dot_tn(a, b):
    return lax.dot_general(a, b, (((0,), (0,)), ((), ())), preferred_element_type=F32)


def lanes(index):
    return pl.ds(pl.multiple_of(index * LANES, LANES), LANES)


def wait_bytes(ref, sem):
    pltpu.make_async_copy(ref, ref, sem).wait()


def put(src, dst, send_sem, recv_sem, device):
    pltpu.make_async_remote_copy(
        src_ref=src,
        dst_ref=dst,
        send_sem=send_sem,
        recv_sem=recv_sem,
        device_id=device,
        device_id_type=MESH,
    ).start()


def image_rows(c):
    return pl.ds(c * TOK, TOK)


def row_sum(values):
    return jnp.sum(values, axis=0, keepdims=True)


def three_parts(values):
    high = values.astype(BF).astype(F32)
    rest = values - high
    mid = rest.astype(BF).astype(F32)
    return high, mid, rest - mid


def kernel(
    images, counts, attn_gain, attn_shift, w_query, b_query, w_key, w_value, b_value, w_out,
    b_out, mlp_gain, mlp_shift, w_up, b_up, w_down, b_down, cotangent,
    act_o, ig_o, g_attn_gain, g_attn_shift, g_w_query, g_b_query, g_w_key, g_w_value, g_b_value,
    g_w_out, g_b_out, g_mlp_gain, g_mlp_shift, g_w_up, g_b_up, g_w_down, g_b_down,
    vec, cot, wqkv, wo, wup, wdn,
    xg, mg, gg, gmg, norm, unit, rstd, res, mid, gcur, gmid,
    stage, rsb, stat, kv, qg, dog, owna, attn_f, attn_b, aux, hid, pre,
    grad_pre, ybuf, igbuf, s_vec, r_vec, vgrad,
    lsem, gy_send, gy_recv, st_send, st_recv, kv_send, kv_recv, do_send, do_recv,
    vec_send, vec_recv, wa1_send, wa1_recv, wa2_send, wa2_recv, wb1_send, wb1_recv, wb2_send,
    wb2_recv, ga1_send, ga1_recv, ga2_send, ga2_recv, gb1_send, gb1_recv, gb2_send, gb2_recv,
    v_send, v_recv, a_send, a_recv, i_send, i_recv, *grad_refs,
):
    staged, ra1, pa, ra2, rb1, pb, rb2 = [grad_refs[4 * n : 4 * n + 4] for n in range(7)]
    weights_at = (wqkv, wo, wup, wdn)
    s = lax.axis_index("section")
    gx = lax.axis_index("gx")
    gy = lax.axis_index("gy")
    other = 1 - s
    mine = lanes(gy)
    x = gx // 2
    h = lax.rem(gx, 2)
    y_slot = h * 2 + s

    barrier = pltpu.get_barrier_semaphore()

    def greet(device):
        pl.semaphore_signal(barrier, inc=1, device_id=device, device_id_type=MESH)

    gy_peers = [(s, gx, lax.rem(gy + k, 8)) for k in range(1, 8)]
    gx_peers = [(s, lax.rem(gx + k, 8), gy) for k in range(1, 8)]
    far_gx = [(other, lax.rem(gx + k, 8), gy) for k in range(8)]
    far_gy = [(other, gx, lax.rem(gy + k, 8)) for k in range(8)]
    x_peers = [(s, lax.rem(x + k, 4) * 2 + h, gy) for k in range(1, 4)]
    y_peers = [(s, x * 2 + 1 - h, gy), (other, gx, gy), (other, x * 2 + 1 - h, gy)]
    for device in gy_peers + gx_peers + far_gx + far_gy[1:]:
        greet(device)

    own = [pltpu.make_async_copy(images.at[s], xg.at[0, :, mine], lsem.at[0])]
    own.append(pltpu.make_async_copy(cotangent.at[s], cot, lsem.at[1]))
    rows = [attn_gain, attn_shift, mlp_gain, mlp_shift, b_query, b_value, b_out, b_down]
    vec_own = []
    for row, ref in enumerate(rows):
        vec_own.append(pltpu.make_async_copy(ref, vec.at[s, row, :, mine], lsem.at[8 + row]))
    for part in range(4):
        vec_own.append(
            pltpu.make_async_copy(
                b_up.at[:, part * LANES : (part + 1) * LANES],
                vec.at[s, V_BU + part, :, mine],
                lsem.at[16 + part],
            )
        )
    w_own = []
    for part, ref in enumerate((w_query, w_key, w_value)):
        w_own.append(
            pltpu.make_async_copy(
                ref, wqkv.at[s, x, h, :, part * LANES : (part + 1) * LANES], lsem.at[2 + part]
            )
        )
    w_own.append(pltpu.make_async_copy(w_out, wo.at[s, x, h], lsem.at[5]))
    w_own.append(pltpu.make_async_copy(w_up, wup.at[s, x, h], lsem.at[6]))
    w_own.append(pltpu.make_async_copy(w_down, wdn.at[s, x, h], lsem.at[7]))
    for copy in own + vec_own + w_own:
        copy.start()

    pl.semaphore_wait(barrier, 29)

    for c in range(2):
        for device in gy_peers:
            put(
                images.at[s, image_rows(c)],
                xg.at[0, image_rows(c), mine],
                gy_send.at[K_X, 0, c],
                gy_recv.at[K_X, 0, c],
                device,
            )
    for copy in vec_own:
        copy.wait()
    for near, group in ((0, gy_peers), (1, far_gy)):
        for device in group:
            block = vec.at[s, :, :, mine]
            put(block, block, vec_send.at[near], vec_recv.at[near], device)
    for copy in w_own:
        copy.wait()
    own[0].wait()
    own[1].wait()

    half_rows = (64, 64, 64, 256)

    def halves(group):
        return pl.ds(0, half_rows[group]), pl.ds(half_rows[group], half_rows[group])

    def spread_own(groups):
        for group in groups:
            ref = weights_at[group]
            first, second = halves(group)
            block = ref.at[s, x, h, first]
            for device in x_peers:
                put(block, block, wa1_send.at[group], wa1_recv.at[group], device)
            block = ref.at[s, x, h, second]
            for device in y_peers:
                put(block, block, wb1_send.at[group], wb1_recv.at[group, s], device)

    def pass_on(groups, l):
        for group in groups:
            ref = weights_at[group]
            first, second = halves(group)

            @pl.when(l == s)
            def _(ref=ref, first=first, group=group):
                wait_bytes(ref.at[l, 0:3, 0, first], wa1_recv.at[group])
                block = ref.at[s, :, h, first]
                for device in y_peers:
                    put(block, block, wa2_send.at[group], wa2_recv.at[group, s], device)
                wait_bytes(ref.at[l, 0, 0, first], wb1_recv.at[group, l])

            @pl.when(l != s)
            def _(ref=ref, first=first, group=group):
                wait_bytes(ref.at[l, 0, :, first], wb1_recv.at[group, l])

            block = ref.at[l, x, :, second]
            for device in x_peers:
                put(block, block, wb2_send.at[group, l], wb2_recv.at[group, l], device)

    def wait_weights(group, l):
        ref = weights_at[group]
        first, _ = halves(group)

        @pl.when(l == s)
        def _():
            wait_bytes(ref.at[l, :, 0, first], wa2_recv.at[group, l])

        @pl.when(l != s)
        def _():
            wait_bytes(ref.at[l, :, :, first], wa2_recv.at[group, l])

        wait_bytes(ref.at[l, 0:3, :, first], wb2_recv.at[group, l])

    def by_columns(ref, l):
        return jnp.concatenate([ref[l, a, b] for a in range(4) for b in range(2)], axis=1)

    @pl.when(s == 0)
    def _():
        spread_own((0, 1, 2, 3))

    def gather_gy(buffer, kind, l, c):
        block = buffer.at[l, image_rows(c), mine]
        for device in gy_peers:
            put(block, block, gy_send.at[kind, l, c], gy_recv.at[kind, l, c], device)

    def wait_gather(buffer, kind, l, c):
        wait_bytes(buffer.at[l, image_rows(c), 0:896], gy_recv.at[kind, l, c])

    slot_of = {K_O: 0, K_D: 1, K_N2: 2, K_N1: 3}

    def scatter_gy(partial, kind, l, c):
        slot = slot_of[kind]
        stage[slot, l, image_rows(c)] = partial.astype(BF)
        for _, _, peer in gy_peers:
            put(
                stage.at[slot, l, image_rows(c), lanes(peer)],
                rsb.at[slot, l, c, gy],
                gy_send.at[kind, l, c],
                gy_recv.at[kind, l, c],
                (s, gx, peer),
            )
        rsb[slot, l, c, gy] = stage[slot, l, image_rows(c), mine]

    def wait_scatter(kind, l, c):
        slot = slot_of[kind]
        wait_bytes(rsb.at[slot, l, c, 0:7], gy_recv.at[kind, l, c])
        total = rsb[slot, l, c, 0].astype(F32)
        for source in range(1, 8):
            total = total + rsb[slot, l, c, source].astype(F32)
        return total

    lane_id = lax.broadcasted_iota(jnp.int32, (TOK, LANES), 1)
    low_half = lane_id < 64
    head_mask = [low_half.astype(F32).astype(BF), (lane_id >= 64).astype(F32).astype(BF)]

    def two_heads(block):
        return jnp.concatenate([block * head_mask[0], block * head_mask[1]], axis=0)

    def join_heads(both):
        return jnp.where(low_half, both[:TOK], both[TOK:])

    def masked_lanes(low, count, value, height):
        ids = lax.broadcasted_iota(jnp.int32, (height, LANES), 1)
        return jnp.where((ids >= low) & (ids < low + count), value, 0.0).astype(BF)

    key_ok = lax.broadcasted_iota(jnp.int32, (ROWS, 640), 1) < SEQ

    def norm_rows(values, gain_row, shift_row, which, l, c):
        center = values - jnp.mean(values, axis=-1, keepdims=True)
        spread = jnp.mean(center * center, axis=-1, keepdims=True)
        scale = lax.rsqrt(spread + EPS)
        xhat = center * scale
        unit[which, l, image_rows(c)] = xhat
        rstd[which, l, image_rows(c)] = jnp.broadcast_to(scale, (TOK, LANES))
        normed = (xhat * vec[l, gain_row] + vec[l, shift_row]).astype(BF)
        norm[which, l, image_rows(c)] = normed
        return normed

    pass_on((0,), 0)

    res[...] = xg[0, :, mine].astype(F32)
    wait_bytes(vec.at[s, :, :, 0:896], vec_recv.at[0])
    wait_bytes(vec.at[other], vec_recv.at[1])

    def forward(l, carry):
        for c in range(2):
            wait_gather(xg, K_X, l, c)
            normed = norm_rows(xg[l, image_rows(c)].astype(F32), V_AG, V_AS, 0, l, c)
            if c == 0:
                wait_weights(0, l)
            qkv = dot_nn(normed, wqkv[l].reshape(WIDE, 384))
            kv[l, 0, c, gx] = qkv[:, LANES : 2 * LANES].astype(BF)
            kv[l, 1, c, gx] = (qkv[:, 2 * LANES :] + vec[l, V_BV, :, mine]).astype(BF)
            query = (qkv[:, :LANES] + vec[l, V_BQ, :, mine]).astype(BF)
            qg[l, c, gx] = query * jnp.asarray(0.125, BF)
            for device in gx_peers:
                block = kv.at[l, :, c, gx]
                put(block, block, kv_send.at[0, l, c], kv_recv.at[0, l, c], device)
        for device in gx_peers:
            block = qg.at[l, :, gx]
            put(block, block, kv_send.at[1, l, 0], kv_recv.at[1, l, 0], device)

        @pl.when(l == 0)
        def _():
            pass_on((1, 2, 3), 0)

            @pl.when(s == 1)
            def _():
                spread_own((0, 1, 2, 3))

        for c in range(2):
            wait_bytes(kv.at[l, :, c, 0:7], kv_recv.at[0, l, c])
            all_keys = kv[l, 0, c].reshape(640, LANES)
            all_values = kv[l, 1, c].reshape(640, LANES)
            scores = dot_nt(two_heads(qg[l, c, gx]), all_keys)
            scores = jnp.where(key_ok, scores, NEG)
            highest = jnp.max(scores, axis=-1, keepdims=True)
            exponent = jnp.exp(scores - highest)
            summed = jnp.sum(exponent, axis=-1, keepdims=True)
            full = exponent / summed
            weights = full.astype(BF)
            mixed = join_heads(dot_nn(weights, all_values))
            mixed_low = mixed.astype(BF)
            attn_b[l, image_rows(c)] = mixed_low
            if c == 0:
                wait_weights(1, l)
            scatter_gy(dot_nn(mixed_low, by_columns(wo, l)), K_O, l, c)
            left_out = (full - weights.astype(F32)).astype(BF)
            attn_f[l, image_rows(c)] = mixed + join_heads(dot_nn(left_out, all_values))
            logs = highest + jnp.log(summed)
            line = jnp.zeros((TOK, LANES), F32)
            for head in range(2):
                for at, piece in enumerate(three_parts(logs[head * TOK : (head + 1) * TOK])):
                    line = jnp.where(lane_id == head * 3 + at, piece, line)
            aux[l, image_rows(c)] = line
        for c in range(2):
            middle = res[image_rows(c)] + wait_scatter(K_O, l, c) + vec[l, V_BO, :, mine]
            mid[image_rows(c)] = middle
            mg[l, image_rows(c), mine] = middle.astype(BF)
            gather_gy(mg, K_M, l, c)
        bias = jnp.concatenate([vec[l, V_BU + n, :, mine] for n in range(4)], axis=1)
        for c in range(2):
            wait_gather(mg, K_M, l, c)
            normed = norm_rows(mg[l, image_rows(c)].astype(F32), V_MG, V_MS, 1, l, c)
            if c == 0:
                wait_weights(2, l)
            pre_act = dot_nn(normed, wup[l].reshape(WIDE, 512)) + bias
            gate = 0.5 * (1.0 + lax.erf(pre_act * 0.7071067811865476))
            hidden = (pre_act * gate).astype(BF)
            hid[l, image_rows(c)] = hidden
            if c == 0:
                wait_weights(3, l)
            scatter_gy(dot_nn(hidden, by_columns(wdn, l)), K_D, l, c)
            slope = jnp.exp(-0.5 * pre_act * pre_act) * 0.3989422804014327
            pre[l, image_rows(c)] = gate + pre_act * slope

        @pl.when(l == 0)
        def _():
            pass_on((0, 1, 2, 3), 1)

        for c in range(2):
            output = mid[image_rows(c)] + wait_scatter(K_D, l, c) + vec[l, V_BD, :, mine]
            output = output.astype(BF)
            ybuf[l, image_rows(c)] = output
            res[image_rows(c)] = output.astype(F32)

            @pl.when(l == 0)
            def _(c=c, output=output):
                xg[1, image_rows(c), mine] = output
                gather_gy(xg, K_X, 1, c)

        @pl.when(l == s)
        def _():
            pltpu.make_async_copy(ybuf.at[l], act_o.at[s], a_recv.at[0]).start()

        @pl.when(l != s)
        def _():
            put(ybuf.at[l], act_o.at[s], a_send.at[0], a_recv.at[0], (other, gx, gy))

        return carry

    lax.fori_loop(0, 2, forward, 0)

    row_id = lax.broadcasted_iota(jnp.int32, (ROWS, LANES), 0)
    image_id = (row_id >= TOK).astype(jnp.int32)
    position = row_id - image_id * TOK + gx * TOK
    live = ((image_id < counts[s]) & (position < SEQ)).astype(F32)
    gcur[...] = cot[...].astype(F32) * live

    def reduce_start(groups, l):
        for group in groups:
            first, second = halves(group)
            ref = staged[group]
            for _, peer, _ in x_peers:
                put(
                    ref.at[l, peer // 2, :, first],
                    ra1[group].at[l, x],
                    ga1_send.at[group, l],
                    ga1_recv.at[group, l],
                    (s, peer, gy),
                )
            put(
                ref.at[l, :, 1 - h, second],
                rb1[group].at[y_slot],
                gb1_send.at[group, l],
                gb1_recv.at[group],
                (l, x * 2 + 1 - h, gy),
            )

            @pl.when(l != s)
            def _(ref=ref, second=second, group=group):
                put(
                    ref.at[l, :, h, second],
                    rb1[group].at[y_slot],
                    gb1_send.at[group, l],
                    gb1_recv.at[group],
                    (l, gx, gy),
                )

            ra1[group][l, x] = ref[l, x, :, first]

            @pl.when(l == s)
            def _(ref=ref, second=second, group=group):
                rb1[group][y_slot] = ref[l, :, h, second]

    def four(ref, index=None):
        parts = [(ref[n] if index is None else ref[index, n]).astype(F32) for n in range(4)]
        return (parts[0] + parts[1]) + (parts[2] + parts[3])

    def reduce_turn(groups, l):
        for group in groups:
            wait_bytes(ra1[group].at[l, 0:3], ga1_recv.at[group, l])
            pa[group][l] = four(ra1[group], l).astype(BF)
            put(
                pa[group].at[l, 1 - h],
                ra2[group].at[y_slot],
                ga2_send.at[group, l],
                ga2_recv.at[group],
                (l, x * 2 + 1 - h, gy),
            )

            @pl.when(l != s)
            def _(group=group):
                put(
                    pa[group].at[l, h],
                    ra2[group].at[y_slot],
                    ga2_send.at[group, l],
                    ga2_recv.at[group],
                    (l, gx, gy),
                )

            @pl.when(l == s)
            def _(group=group):
                ra2[group][y_slot] = pa[group][l, h]
                wait_bytes(rb1[group].at[0:3], gb1_recv.at[group])
                pb[group][...] = four(rb1[group]).astype(BF)
                for _, peer, _ in x_peers:
                    put(
                        pb[group].at[peer // 2],
                        rb2[group].at[x],
                        gb2_send.at[group],
                        gb2_recv.at[group],
                        (s, peer, gy),
                    )
                rb2[group][x] = pb[group][x]

    def send_vec(l):
        for j in range(8):
            k = lax.rem(gx + j, 8)
            dst = r_vec.at[s * 8 + gx]
            if j == 0:

                @pl.when(l == s)
                def _():
                    r_vec[s * 8 + gx] = s_vec[l]

                @pl.when(l != s)
                def _(k=k):
                    put(s_vec.at[l], r_vec.at[s * 8 + gx], v_send.at[l], v_recv.at[0], (l, k, gy))

            else:
                put(s_vec.at[l], dst, v_send.at[l], v_recv.at[0], (l, k, gy))

    def send_stats(first, second, which, l, c):
        ids = lax.broadcasted_iota(jnp.int32, (TOK, LANES), 1)
        both = jnp.where(ids == 0, first, jnp.where(ids == 1, second, 0.0))
        both = jnp.concatenate([both, jnp.zeros((LANES - TOK, LANES), F32)], axis=0)
        stat[which, l, c, gy] = both.T[:8]
        for device in gy_peers:
            block = stat.at[which, l, c, gy]
            put(block, block, st_send.at[which, l, c], st_recv.at[which, l, c], device)

    def wait_stats(which, l, c):
        wait_bytes(stat.at[which, l, c, 0:7], st_recv.at[which, l, c])
        total = stat[which, l, c, 0]
        for source in range(1, 8):
            total = total + stat[which, l, c, source]
        total = jnp.concatenate([total, jnp.zeros((LANES - 8, LANES), F32)], axis=0).T
        return total[:TOK, 0:1], total[:TOK, 1:2]

    def norm_back_send(partial, which, gain_row, kind, l, c):
        scatter_gy(partial, kind, l, c)
        weighted = partial * vec[l, gain_row]
        first = jnp.sum(weighted, axis=-1, keepdims=True)
        second = jnp.sum(weighted * unit[which, l, image_rows(c)], axis=-1, keepdims=True)
        send_stats(first, second, which, l, c)

    def add_vec(slot, value, c):
        if c == 0:
            vgrad[slot] = value
        else:
            vgrad[slot] += value

    def norm_back_take(which, gain_row, kind, l, c, gain_slot, shift_slot):
        grad = wait_scatter(kind, l, c)
        first, second = wait_stats(which, l, c)
        xhat = unit[which, l, image_rows(c), mine]
        add_vec(gain_slot, row_sum(grad * xhat), c)
        add_vec(shift_slot, row_sum(grad), c)
        inner = grad * vec[l, gain_row, :, mine]
        return rstd[which, l, image_rows(c)] * (
            inner - first * (1.0 / WIDE) - xhat * (second * (1.0 / WIDE))
        )

    def store_columns(group, grad, l):
        for block in range(8):
            columns = grad[:, block * LANES : (block + 1) * LANES]
            staged[group][l, block // 2, block % 2] = columns.astype(BF)

    def start_gradient(l, c):
        grad_out = gcur[image_rows(c)]
        gg[l, image_rows(c), mine] = grad_out.astype(BF)
        gather_gy(gg, K_G, l, c)

    key_side = masked_lanes(0, 6, -1.0, 640)
    value_side = masked_lanes(6, 6, -1.0, 640)
    row_ids = lax.broadcasted_iota(jnp.int32, (ROWS, 640), 0)
    key_pos = jnp.where(row_ids >= TOK, row_ids - TOK, row_ids) + gx * TOK
    own_ok = key_pos < SEQ
    for c in range(2):
        start_gradient(1, c)

    def backward(step, carry):
        l = 1 - step
        vgrad[V_BD] = row_sum(gcur[...])
        for c in range(2):
            wait_gather(gg, K_G, l, c)
            grad_hid = dot_nt(gg[l, image_rows(c)], by_columns(wdn, l))
            low = (grad_hid * pre[l, image_rows(c)]).astype(BF)
            grad_pre[image_rows(c)] = low
            norm_back_send(
                dot_nt(low, wup[l].reshape(WIDE, 512)), 1, V_MG, K_N2, l, c
            )
        up_sum = row_sum(grad_pre[...].astype(F32))
        for n in range(4):
            vgrad[V_BU + n] = up_sum[:, n * LANES : (n + 1) * LANES]
        store_columns(3, dot_tn(hid[l], gg[l]), l)
        for c in range(2):
            grad_mid = gcur[image_rows(c)] + norm_back_take(1, V_MG, K_N2, l, c, V_MG, V_MS)
            gmid[image_rows(c)] = grad_mid
            gmg[l, image_rows(c), mine] = grad_mid.astype(BF)
            gather_gy(gmg, K_GM, l, c)
        staged[2][l] = dot_tn(norm[1, l], grad_pre[...]).astype(BF).reshape(4, 2, LANES, 512)
        vgrad[V_BO] = row_sum(gmid[...])
        for c in range(2):
            wait_gather(gmg, K_GM, l, c)
            grad_mixed = dot_nt(gmg[l, image_rows(c)], by_columns(wo, l)).astype(BF)
            product = grad_mixed.astype(F32) * attn_f[l, image_rows(c)]
            line = aux[l, image_rows(c)]
            for head in range(2):
                picked = jnp.where(low_half == (head == 0), product, 0.0)
                delta = jnp.sum(picked, axis=-1, keepdims=True)
                for at, piece in enumerate(three_parts(delta)):
                    line = jnp.where(lane_id == 6 + head * 3 + at, piece, line)
            dog[l, c, gx, :, 0:LANES] = grad_mixed
            dog[l, c, gx, :, LANES:] = line.astype(BF)
            for device in gx_peers:
                block = dog.at[l, c, gx]
                put(block, block, do_send.at[l, c], do_recv.at[l, c], device)
        store_columns(1, dot_tn(attn_b[l], gmg[l]), l)
        reduce_start((3, 2, 1), l)

        @pl.when(l == 1)
        def _():
            wait_bytes(qg.at[0, :, 0:7], kv_recv.at[1, 0, 0])
            wait_bytes(qg.at[1, :, 0:7], kv_recv.at[1, 1, 0])

        for c in range(2):
            wait_bytes(dog.at[l, c, 0:7], do_recv.at[l, c])
            all_keys = kv[l, 0, c].reshape(640, LANES)
            all_values = kv[l, 1, c].reshape(640, LANES)
            all_query = qg[l, c].reshape(640, LANES)
            all_grads = dog[l, c].reshape(640, 2 * LANES)
            all_aux = all_grads[:, LANES:]
            all_mixed = all_grads[:, :LANES]
            my_aux = dog[l, c, gx, :, LANES:]
            my_log = jnp.concatenate(
                [my_aux * masked_lanes(0, 3, 1.0, TOK), my_aux * masked_lanes(3, 3, 1.0, TOK)],
                axis=0,
            )
            my_delta = jnp.concatenate(
                [my_aux * masked_lanes(6, 3, 1.0, TOK), my_aux * masked_lanes(9, 3, 1.0, TOK)],
                axis=0,
            )
            my_query = jnp.concatenate([two_heads(qg[l, c, gx]), my_log], axis=1)
            my_mixed = jnp.concatenate([two_heads(dog[l, c, gx, :, 0:LANES]), my_delta], axis=1)
            scores = dot_nt(my_query, jnp.concatenate([all_keys, key_side], axis=1))
            weights = jnp.exp(jnp.where(key_ok, scores, NEG))
            inner = dot_nt(my_mixed, jnp.concatenate([all_values, value_side], axis=1))
            grad_scores = (weights * inner).astype(BF)
            grad_query = join_heads(dot_nn(grad_scores, all_keys)) * 0.125
            owna[image_rows(c), 0:LANES] = grad_query.astype(BF)

            key_log = jnp.concatenate(
                [masked_lanes(0, 3, -1.0, TOK), masked_lanes(3, 3, -1.0, TOK)], axis=0
            )
            key_delta = jnp.concatenate(
                [masked_lanes(6, 3, -1.0, TOK), masked_lanes(9, 3, -1.0, TOK)], axis=0
            )
            my_key = jnp.concatenate([two_heads(kv[l, 0, c, gx]), key_log], axis=1)
            my_value = jnp.concatenate([two_heads(kv[l, 1, c, gx]), key_delta], axis=1)
            scores = dot_nt(my_key, jnp.concatenate([all_query, all_aux], axis=1))
            weights = jnp.exp(jnp.where(own_ok, scores, NEG))
            inner = dot_nt(my_value, all_grads)
            grad_scores = (weights * inner).astype(BF)
            grad_key = join_heads(dot_nn(grad_scores, all_query))
            grad_value = join_heads(dot_nn(weights.astype(BF), all_mixed))
            owna[image_rows(c), LANES : 2 * LANES] = grad_key.astype(BF)
            owna[image_rows(c), 2 * LANES :] = grad_value.astype(BF)
            norm_back_send(
                dot_nt(owna[image_rows(c)], wqkv[l].reshape(WIDE, 384)), 0, V_AG, K_N1, l, c
            )
        staged[0][l] = dot_tn(norm[0, l], owna[...]).astype(BF).reshape(4, 2, LANES, 384)
        reduce_start((0,), l)
        bias_sum = row_sum(owna[...].astype(F32))
        vgrad[V_BQ] = bias_sum[:, :LANES]
        vgrad[V_BV] = bias_sum[:, 2 * LANES :]
        for c in range(2):
            grad_in = gmid[image_rows(c)] + norm_back_take(0, V_AG, K_N1, l, c, V_AG, V_AS)
            igbuf[l, image_rows(c)] = grad_in
            gcur[image_rows(c)] = grad_in.astype(BF).astype(F32)

            @pl.when(l == 1)
            def _(c=c):
                start_gradient(0, c)

        s_vec[l] = vgrad[...]
        send_vec(l)

        @pl.when(l == s)
        def _():
            pltpu.make_async_copy(igbuf.at[l], ig_o.at[s], i_recv.at[0]).start()

        @pl.when(l != s)
        def _():
            put(igbuf.at[l], ig_o.at[s], i_send.at[0], i_recv.at[0], (other, gx, gy))

        reduce_turn((3, 2, 1, 0), l)
        return carry

    lax.fori_loop(0, 2, backward, 0)

    def sum_of(ref):
        total = ref[0].astype(F32)
        for source in range(1, 16):
            total = total + ref[source].astype(F32)
        return total

    def final_sum(group):
        first, second = halves(group)
        wait_bytes(ra2[group].at[0:3], ga2_recv.at[group])
        wait_bytes(rb2[group].at[0:3], gb2_recv.at[group])
        return jnp.concatenate([four(ra2[group]), four(rb2[group])], axis=0)

    g_w_down[...] = final_sum(3)
    g_w_up[...] = final_sum(2)
    g_w_out[...] = final_sum(1)
    total = final_sum(0)
    g_w_query[...] = total[:, :LANES]
    g_w_key[...] = total[:, LANES : 2 * LANES]
    g_w_value[...] = total[:, 2 * LANES :]
    wait_bytes(r_vec.at[0:15], v_recv.at[0])
    total = sum_of(r_vec)
    g_attn_gain[...] = total[V_AG]
    g_attn_shift[...] = total[V_AS]
    g_mlp_gain[...] = total[V_MG]
    g_mlp_shift[...] = total[V_MS]
    g_b_query[...] = total[V_BQ]
    g_b_value[...] = total[V_BV]
    g_b_out[...] = total[V_BO]
    g_b_down[...] = total[V_BD]
    for part in range(4):
        g_b_up[:, part * LANES : (part + 1) * LANES] = total[V_BU + part]
    wait_bytes(act_o, a_recv.at[0])
    wait_bytes(ig_o, i_recv.at[0])

    wait_bytes(ybuf.at[0], a_send.at[0])
    wait_bytes(igbuf.at[0], i_send.at[0])
    wait_bytes(vec.at[s, :, :, 0:896], vec_send.at[0])
    wait_bytes(vec.at[s], vec_send.at[1])
    for group in range(4):
        ref = weights_at[group]
        first, _ = halves(group)
        wait_bytes(ref.at[0, 0:3, 0, first], wa1_send.at[group])
        wait_bytes(ref.at[0, 0:3, 0, first], wb1_send.at[group])
        wait_bytes(ref.at[0, 0:3], wa2_send.at[group])
        wait_bytes(rb2[group].at[0:3], gb2_send.at[group])
        for l in range(2):
            wait_bytes(ref.at[0, 0:3, :, first], wb2_send.at[group, l])
            wait_bytes(ra1[group].at[l, 0:3], ga1_send.at[group, l])
    for l in range(2):
        for c in range(2):
            for kind, buffer in ((K_X, xg), (K_M, mg), (K_G, gg), (K_GM, gmg)):
                wait_bytes(buffer.at[l, image_rows(c), 0:896], gy_send.at[kind, l, c])
            for kind, slot in slot_of.items():
                wait_bytes(rsb.at[slot, l, c, 0:7], gy_send.at[kind, l, c])
            for which in range(2):
                wait_bytes(stat.at[which, l, c, 0:7], st_send.at[which, l, c])
            wait_bytes(kv.at[l, :, c, 0:7], kv_send.at[0, l, c])
            wait_bytes(dog.at[l, c, 0:7], do_send.at[l, c])
        wait_bytes(qg.at[l, :, 0:7], kv_send.at[1, l, 0])
        for count, at in ((1, l), (2, 1 - l)):

            @pl.when(s == at)
            def _(l=l, count=count):
                for group in range(4):
                    wait_bytes(ra2[group].at[0:count], ga2_send.at[group, l])
                    wait_bytes(rb1[group].at[0:count], gb1_send.at[group, l])
                wait_bytes(r_vec.at[0 : 6 + count], v_send.at[l])


def write_out(*refs):
    copies = [
        pltpu.make_async_copy(refs[n], refs[17 + n], refs[34].at[n]) for n in range(17)
    ]
    for copy in copies:
        copy.start()
    for copy in copies:
        copy.wait()


def finish(values):
    return pl.pallas_call(
        write_out,
        out_shape=[jax.ShapeDtypeStruct(value.shape, value.dtype) for value in values],
        in_specs=[pl.BlockSpec(memory_space=pltpu.VMEM)] * 17,
        out_specs=[pl.BlockSpec(memory_space=pl.ANY)] * 17,
        scratch_shapes=[pltpu.SemaphoreType.DMA((17,))],
        name="write_results",
    )(*values)


def local(
    images, counts, attn_gain, attn_shift, w_query, b_query, w_key, w_value, b_value, w_out,
    b_out, mlp_gain, mlp_shift, w_up, b_up, w_down, b_down, cotangent,
):
    anywhere = pl.BlockSpec(memory_space=pl.ANY)
    in_vmem = pl.BlockSpec(memory_space=pltpu.VMEM)
    in_smem = pl.BlockSpec(memory_space=pltpu.SMEM)
    in_specs = [anywhere, in_smem] + [anywhere] * 16
    row = jax.ShapeDtypeStruct((1, LANES), F32)
    square = jax.ShapeDtypeStruct((LANES, LANES), F32)
    out_shape = [
        jax.ShapeDtypeStruct((2, ROWS, LANES), BF),
        jax.ShapeDtypeStruct((2, ROWS, LANES), F32),
        row, row, square, row, square, square, row, square, row, row, row,
        jax.ShapeDtypeStruct((LANES, 512), F32),
        jax.ShapeDtypeStruct((1, 512), F32),
        jax.ShapeDtypeStruct((512, LANES), F32),
        row,
    ]
    vmem = pltpu.VMEM
    scratch = [
        vmem((2, 12, 1, WIDE), F32),
        vmem((ROWS, LANES), BF),
        vmem((2, 4, 2, LANES, 384), BF),
        vmem((2, 4, 2, LANES, LANES), BF),
        vmem((2, 4, 2, LANES, 512), BF),
        vmem((2, 4, 2, 512, LANES), BF),
        vmem((2, ROWS, WIDE), BF),
        vmem((2, ROWS, WIDE), BF),
        vmem((2, ROWS, WIDE), BF),
        vmem((2, ROWS, WIDE), BF),
        vmem((2, 2, ROWS, WIDE), BF),
        vmem((2, 2, ROWS, WIDE), F32),
        vmem((2, 2, ROWS, LANES), F32),
        vmem((ROWS, LANES), F32),
        vmem((ROWS, LANES), F32),
        vmem((ROWS, LANES), F32),
        vmem((ROWS, LANES), F32),
        vmem((4, 2, ROWS, WIDE), BF),
        vmem((4, 2, 2, 8, TOK, LANES), BF),
        vmem((2, 2, 2, 8, 8, LANES), F32),
        vmem((2, 2, 2, 8, TOK, LANES), BF),
        vmem((2, 2, 8, TOK, LANES), BF),
        vmem((2, 2, 8, TOK, 2 * LANES), BF),
        vmem((ROWS, 384), BF),
        vmem((2, ROWS, LANES), F32),
        vmem((2, ROWS, LANES), BF),
        vmem((2, ROWS, LANES), F32),
        vmem((2, ROWS, 512), BF),
        vmem((2, ROWS, 512), F32),
        vmem((ROWS, 512), BF),
        vmem((2, ROWS, LANES), BF),
        vmem((2, ROWS, LANES), F32),
        vmem((2, 12, 1, LANES), F32),
        vmem((16, 12, 1, LANES), F32),
        vmem((12, 1, LANES), F32),
        pltpu.SemaphoreType.DMA((20,)),
        pltpu.SemaphoreType.DMA((8, 2, 2)),
        pltpu.SemaphoreType.DMA((8, 2, 2)),
        pltpu.SemaphoreType.DMA((2, 2, 2)),
        pltpu.SemaphoreType.DMA((2, 2, 2)),
        pltpu.SemaphoreType.DMA((2, 2, 2)),
        pltpu.SemaphoreType.DMA((2, 2, 2)),
        pltpu.SemaphoreType.DMA((2, 2)),
        pltpu.SemaphoreType.DMA((2, 2)),
        pltpu.SemaphoreType.DMA((2,)),
        pltpu.SemaphoreType.DMA((2,)),
        pltpu.SemaphoreType.DMA((4,)),
        pltpu.SemaphoreType.DMA((4,)),
        pltpu.SemaphoreType.DMA((4,)),
        pltpu.SemaphoreType.DMA((4, 2)),
        pltpu.SemaphoreType.DMA((4,)),
        pltpu.SemaphoreType.DMA((4, 2)),
        pltpu.SemaphoreType.DMA((4, 2)),
        pltpu.SemaphoreType.DMA((4, 2)),
        pltpu.SemaphoreType.DMA((4, 2)),
        pltpu.SemaphoreType.DMA((4, 2)),
        pltpu.SemaphoreType.DMA((4, 2)),
        pltpu.SemaphoreType.DMA((4,)),
        pltpu.SemaphoreType.DMA((4, 2)),
        pltpu.SemaphoreType.DMA((4,)),
        pltpu.SemaphoreType.DMA((4,)),
        pltpu.SemaphoreType.DMA((4,)),
        pltpu.SemaphoreType.DMA((2,)),
        pltpu.SemaphoreType.DMA((1,)),
        pltpu.SemaphoreType.DMA((1,)),
        pltpu.SemaphoreType.DMA((1,)),
        pltpu.SemaphoreType.DMA((1,)),
        pltpu.SemaphoreType.DMA((1,)),
    ]
    halved = [(64, 384), (64, LANES), (64, 512), (256, LANES)]
    for lead in (None, (2, 4, 2), (2, 2), (4,), (4, 4), (4,), (4,)):
        for rows, columns in halved:
            if lead is None:
                scratch.append(vmem((2, 4, 2, 2 * rows, columns), BF))
            else:
                scratch.append(vmem(lead + (rows, columns), BF))
    outs = pl.pallas_call(
        kernel,
        out_shape=out_shape,
        in_specs=in_specs,
        out_specs=[in_vmem] * 17,
        scratch_shapes=scratch,
        compiler_params=pltpu.CompilerParams(
            collective_id=0, has_side_effects=True, vmem_limit_bytes=58 * 1024 * 1024
        ),
        cost_estimate=pl.CostEstimate(
            flops=4_000_000_000, bytes_accessed=8_000_000, transcendentals=4_000_000
        ),
        name="two_sections",
    )(
        images.reshape(2, ROWS, LANES), counts, attn_gain, attn_shift, w_query[0], b_query,
        w_key[0], w_value[0], b_value, w_out[0], b_out, mlp_gain, mlp_shift, w_up[0], b_up,
        w_down[0], b_down, cotangent.reshape(2, ROWS, LANES),
    )
    outs = list(finish(outs))
    shape = (1,) + images.shape
    outs[0] = outs[0].reshape(shape)
    outs[1] = outs[1].reshape(shape)
    for index in (4, 6, 7, 9, 13, 15):
        outs[index] = outs[index][None]
    return tuple(outs)


def solution(mesh):
    vector = P("section", "gy")
    in_block = P("section", "gx", "gy")
    out_block = P("section", "gy", "gx")
    rows = P(None, None, "gx", "gy")
    in_specs = (
        rows, P(), vector, vector, in_block, vector, in_block, in_block, vector, out_block,
        vector, vector, vector, in_block, vector, out_block, vector, rows,
    )
    results = P("section", None, None, "gx", "gy")
    out_specs = (
        results, results, vector, vector, in_block, vector, in_block, in_block, vector,
        out_block, vector, vector, vector, in_block, vector, out_block, vector,
    )
    return jax.shard_map(local, mesh=mesh, in_specs=in_specs, out_specs=out_specs, check_vma=False)
```

time: 320 us -> 231 us (0.72)
  Pallas kernels: 308 us -> 230 us
  local copies, waits for them, and re-layouts: 11.3 us -> 0 us
    pallas_call x1, Pallas kernels: 308 us -> 227 us  [local(): pl.pallas_call(kernel, out_shape=out_shape, in_specs=in_specs, out_specs=...]
    unnamed x49 -> x0, local copies, waits for them, and re-layouts: 11.3 us -> none
where the time goes in v2:
time: 231 us
  Pallas kernels  230 us (100%)
    pallas_call x1, Pallas kernels, local(): pl.pallas_call(kernel, out_shape=out_shape, in_specs=in_specs, out_specs=...  227 us

profile of v2, /device:TPU:1, one launch (start us, length us, event | category | flops | bytes accessed | tf_op | source)
XLA Modules:
  0.0 230.5 jit_solution(10875056303722733417)
XLA Ops:
  0.7 227.5 %two_sections.1 = (bf16[2,160,128]{2,1,0:T(8,128)(2,1)}, f32[2,160,128]{2,1,0:T(8,128)}, f32[1,128]{1,0:T(1,128)}, f32[1,128]{1,0:T(1,128)}, f32[128,128]{1,0:T(...) custom-call(bf16[2,160,128]{2,1,0:T(8,128)(2,1)} %bitcast.21, ...), custom_call_target="tpu_custom_call" | custom-call | flops 4000000000 | bytes 8000000 | tf_op jit(solution)/shard_map/two_sections/pallas_call | solution.py:844
  228.1 2.4 %write_results.1 = (bf16[2,160,128]{2,1,0:T(8,128)(2,1)}, f32[2,160,128]{2,1,0:T(8,128)}, f32[1,128]{1,0:T(1,128)}, f32[1,128]{1,0:T(1,128)}, f32[128,128]{1,0:T...) custom-call(bf16[2,160,128]{2,1,0:T(8,128)(2,1)} %get-tuple-element., ...), custom_call_target="tpu_custom_call" | custom-call | tf_op jit(solution)/shard_map/write_results/pallas_call | solution.py:737

commit v3 on v2

--- a/solution.py
+++ b/solution.py
@@ -96,11 +96,14 @@
     def greet(device):
         pl.semaphore_signal(barrier, inc=1, device_id=device, device_id_type=MESH)
 
-    gy_peers = [(s, gx, lax.rem(gy + k, 8)) for k in range(1, 8)]
-    gx_peers = [(s, lax.rem(gx + k, 8), gy) for k in range(1, 8)]
+    gy_peers = [(s, gx, lax.rem(gy + k, 8)) for k in (4, 5, 3, 6, 2, 7, 1)]
     far_gx = [(other, lax.rem(gx + k, 8), gy) for k in range(8)]
     far_gy = [(other, gx, lax.rem(gy + k, 8)) for k in range(8)]
-    x_peers = [(s, lax.rem(x + k, 4) * 2 + h, gy) for k in range(1, 4)]
+    x_peers = [(s, lax.rem(x + k, 4) * 2 + h, gy) for k in (2, 1, 3)]
+    gx_peers = [
+        (s, lax.rem(x + k, 4) * 2 + side, gy)
+        for k, side in ((2, 1 - h), (1, 1 - h), (3, 1 - h), (2, h), (0, 1 - h), (1, h), (3, h))
+    ]
     y_peers = [(s, x * 2 + 1 - h, gy), (other, gx, gy), (other, x * 2 + 1 - h, gy)]
     for device in gy_peers + gx_peers + far_gx + far_gy[1:]:
         greet(device)
@@ -208,9 +211,7 @@
     def by_columns(ref, l):
         return jnp.concatenate([ref[l, a, b] for a in range(4) for b in range(2)], axis=1)
 
-    @pl.when(s == 0)
-    def _():
-        spread_own((0, 1, 2, 3))
+    spread_own((0, 1, 2, 3))
 
     def gather_gy(buffer, kind, l, c):
         block = buffer.at[l, image_rows(c), mine]
@@ -270,17 +271,49 @@
         norm[which, l, image_rows(c)] = normed
         return normed
 
-    pass_on((0,), 0)
+    row_id = lax.broadcasted_iota(jnp.int32, (ROWS, LANES), 0)
+    image_id = (row_id >= TOK).astype(jnp.int32)
+    position = row_id - image_id * TOK + gx * TOK
+    live = ((image_id < counts[s]) & (position < SEQ)).astype(F32)
+    gcur[...] = cot[...].astype(F32) * live
+
+    def start_gradient(l, c):
+        grad_out = gcur[image_rows(c)]
+        gg[l, image_rows(c), mine] = grad_out.astype(BF)
+        gather_gy(gg, K_G, l, c)
 
     res[...] = xg[0, :, mine].astype(F32)
     wait_bytes(vec.at[s, :, :, 0:896], vec_recv.at[0])
     wait_bytes(vec.at[other], vec_recv.at[1])
 
+    def finish_layer(l):
+        for c in range(2):
+            output = mid[image_rows(c)] + wait_scatter(K_D, l, c) + vec[l, V_BD, :, mine]
+            output = output.astype(BF)
+            ybuf[l, image_rows(c)] = output
+            if l == 0:
+                res[image_rows(c)] = output.astype(F32)
+                xg[1, image_rows(c), mine] = output
+                gather_gy(xg, K_X, 1, c)
+
+        @pl.when(s == l)
+        def _():
+            pltpu.make_async_copy(ybuf.at[l], act_o.at[s], a_recv.at[0]).start()
+
+        @pl.when(s != l)
+        def _():
+            put(ybuf.at[l], act_o.at[s], a_send.at[0], a_recv.at[0], (other, gx, gy))
+
     def forward(l, carry):
         for c in range(2):
             wait_gather(xg, K_X, l, c)
             normed = norm_rows(xg[l, image_rows(c)].astype(F32), V_AG, V_AS, 0, l, c)
             if c == 0:
+
+                @pl.when(l == 0)
+                def _():
+                    pass_on((0,), 0)
+
                 wait_weights(0, l)
             qkv = dot_nn(normed, wqkv[l].reshape(WIDE, 384))
             kv[l, 0, c, gx] = qkv[:, LANES : 2 * LANES].astype(BF)
@@ -298,9 +331,10 @@
         def _():
             pass_on((1, 2, 3), 0)
 
-            @pl.when(s == 1)
-            def _():
-                spread_own((0, 1, 2, 3))
+        @pl.when(l == 1)
+        def _():
+            for c in range(2):
+                start_gradient(1, c)
 
         for c in range(2):
             wait_bytes(kv.at[l, :, c, 0:7], kv_recv.at[0, l, c])
@@ -327,11 +361,21 @@
                 for at, piece in enumerate(three_parts(logs[head * TOK : (head + 1) * TOK])):
                     line = jnp.where(lane_id == head * 3 + at, piece, line)
             aux[l, image_rows(c)] = line
+
+        @pl.when(l == 0)
+        def _():
+            pass_on((0, 1), 1)
+
         for c in range(2):
             middle = res[image_rows(c)] + wait_scatter(K_O, l, c) + vec[l, V_BO, :, mine]
             mid[image_rows(c)] = middle
             mg[l, image_rows(c), mine] = middle.astype(BF)
             gather_gy(mg, K_M, l, c)
+
+        @pl.when(l == 0)
+        def _():
+            pass_on((2, 3), 1)
+
         bias = jnp.concatenate([vec[l, V_BU + n, :, mine] for n in range(4)], axis=1)
         for c in range(2):
             wait_gather(mg, K_M, l, c)
@@ -350,36 +394,11 @@
 
         @pl.when(l == 0)
         def _():
-            pass_on((0, 1, 2, 3), 1)
-
-        for c in range(2):
-            output = mid[image_rows(c)] + wait_scatter(K_D, l, c) + vec[l, V_BD, :, mine]
-            output = output.astype(BF)
-            ybuf[l, image_rows(c)] = output
-            res[image_rows(c)] = output.astype(F32)
-
-            @pl.when(l == 0)
-            def _(c=c, output=output):
-                xg[1, image_rows(c), mine] = output
-                gather_gy(xg, K_X, 1, c)
-
-        @pl.when(l == s)
-        def _():
-            pltpu.make_async_copy(ybuf.at[l], act_o.at[s], a_recv.at[0]).start()
-
-        @pl.when(l != s)
-        def _():
-            put(ybuf.at[l], act_o.at[s], a_send.at[0], a_recv.at[0], (other, gx, gy))
+            finish_layer(0)
 
         return carry
 
     lax.fori_loop(0, 2, forward, 0)
-
-    row_id = lax.broadcasted_iota(jnp.int32, (ROWS, LANES), 0)
-    image_id = (row_id >= TOK).astype(jnp.int32)
-    position = row_id - image_id * TOK + gx * TOK
-    live = ((image_id < counts[s]) & (position < SEQ)).astype(F32)
-    gcur[...] = cot[...].astype(F32) * live
 
     def reduce_start(groups, l):
         for group in groups:
@@ -521,19 +540,11 @@
             columns = grad[:, block * LANES : (block + 1) * LANES]
             staged[group][l, block // 2, block % 2] = columns.astype(BF)
 
-    def start_gradient(l, c):
-        grad_out = gcur[image_rows(c)]
-        gg[l, image_rows(c), mine] = grad_out.astype(BF)
-        gather_gy(gg, K_G, l, c)
-
     key_side = masked_lanes(0, 6, -1.0, 640)
     value_side = masked_lanes(6, 6, -1.0, 640)
     row_ids = lax.broadcasted_iota(jnp.int32, (ROWS, 640), 0)
     key_pos = jnp.where(row_ids >= TOK, row_ids - TOK, row_ids) + gx * TOK
     own_ok = key_pos < SEQ
-    for c in range(2):
-        start_gradient(1, c)
-
     def backward(step, carry):
         l = 1 - step
         vgrad[V_BD] = row_sum(gcur[...])
@@ -549,12 +560,23 @@
         for n in range(4):
             vgrad[V_BU + n] = up_sum[:, n * LANES : (n + 1) * LANES]
         store_columns(3, dot_tn(hid[l], gg[l]), l)
+        reduce_start((3,), l)
+
+        @pl.when(l == 0)
+        def _():
+            reduce_turn((0,), 1)
+
+        @pl.when(l == 1)
+        def _():
+            finish_layer(1)
+
         for c in range(2):
             grad_mid = gcur[image_rows(c)] + norm_back_take(1, V_MG, K_N2, l, c, V_MG, V_MS)
             gmid[image_rows(c)] = grad_mid
             gmg[l, image_rows(c), mine] = grad_mid.astype(BF)
             gather_gy(gmg, K_GM, l, c)
         staged[2][l] = dot_tn(norm[1, l], grad_pre[...]).astype(BF).reshape(4, 2, LANES, 512)
+        reduce_start((2,), l)
         vgrad[V_BO] = row_sum(gmid[...])
         for c in range(2):
             wait_gather(gmg, K_GM, l, c)
@@ -572,7 +594,8 @@
                 block = dog.at[l, c, gx]
                 put(block, block, do_send.at[l, c], do_recv.at[l, c], device)
         store_columns(1, dot_tn(attn_b[l], gmg[l]), l)
-        reduce_start((3, 2, 1), l)
+        reduce_start((1,), l)
+        reduce_turn((3,), l)
 
         @pl.when(l == 1)
         def _():
@@ -626,6 +649,7 @@
             )
         staged[0][l] = dot_tn(norm[0, l], owna[...]).astype(BF).reshape(4, 2, LANES, 384)
         reduce_start((0,), l)
+        reduce_turn((2, 1), l)
         bias_sum = row_sum(owna[...].astype(F32))
         vgrad[V_BQ] = bias_sum[:, :LANES]
         vgrad[V_BV] = bias_sum[:, 2 * LANES :]
@@ -649,7 +673,10 @@
         def _():
             put(igbuf.at[l], ig_o.at[s], i_send.at[0], i_recv.at[0], (other, gx, gy))
 
-        reduce_turn((3, 2, 1, 0), l)
+        @pl.when(l == 0)
+        def _():
+            reduce_turn((0,), 0)
+
         return carry
 
     lax.fori_loop(0, 2, backward, 0)

time: 231 us -> 195 us (0.84)
  Pallas kernels: 230 us -> 194 us
    pallas_call x1, Pallas kernels: 227 us -> 191 us  [local(): pl.pallas_call(kernel, out_shape=out_shape, in_specs=in_specs, out_specs=...]
where the time goes in v3:
time: 195 us; the launch traced here: 194 us
  Pallas kernels  194 us (99%)
    pallas_call x1, Pallas kernels, local(): pl.pallas_call(kernel, out_shape=out_shape, in_specs=in_specs, out_specs=...  191 us

profile of v3, /device:TPU:1, one launch (start us, length us, event | category | flops | bytes accessed | tf_op | source)
XLA Modules:
  0.0 194.5 jit_solution(12530155258234635756)
XLA Ops:
  0.7 191.4 %two_sections.1 = (bf16[2,160,128]{2,1,0:T(8,128)(2,1)}, f32[2,160,128]{2,1,0:T(8,128)}, f32[1,128]{1,0:T(1,128)}, f32[1,128]{1,0:T(1,128)}, f32[128,128]{1,0:T(...) custom-call(bf16[2,160,128]{2,1,0:T(8,128)(2,1)} %bitcast.21, ...), custom_call_target="tpu_custom_call" | custom-call | flops 4000000000 | bytes 8000000 | tf_op jit(solution)/shard_map/two_sections/pallas_call | solution.py:871
  192.0 2.4 %write_results.1 = (bf16[2,160,128]{2,1,0:T(8,128)(2,1)}, f32[2,160,128]{2,1,0:T(8,128)}, f32[1,128]{1,0:T(1,128)}, f32[1,128]{1,0:T(1,128)}, f32[128,128]{1,0:T...) custom-call(bf16[2,160,128]{2,1,0:T(8,128)(2,1)} %get-tuple-element., ...), custom_call_target="tpu_custom_call" | custom-call | tf_op jit(solution)/shard_map/write_results/pallas_call | solution.py:764

commit v4 on v3

--- a/solution.py
+++ b/solution.py
@@ -211,7 +211,9 @@
     def by_columns(ref, l):
         return jnp.concatenate([ref[l, a, b] for a in range(4) for b in range(2)], axis=1)
 
-    spread_own((0, 1, 2, 3))
+    @pl.when(s == 0)
+    def _():
+        spread_own((0, 1))
 
     def gather_gy(buffer, kind, l, c):
         block = buffer.at[l, image_rows(c), mine]
@@ -314,6 +316,15 @@
                 def _():
                     pass_on((0,), 0)
 
+                    @pl.when(s == 0)
+                    def _():
+                        spread_own((2, 3))
+
+                    @pl.when(s == 1)
+                    def _():
+                        spread_own((0, 1, 2, 3))
+
+
                 wait_weights(0, l)
             qkv = dot_nn(normed, wqkv[l].reshape(WIDE, 384))
             kv[l, 0, c, gx] = qkv[:, LANES : 2 * LANES].astype(BF)
@@ -323,19 +334,21 @@
             for device in gx_peers:
                 block = kv.at[l, :, c, gx]
                 put(block, block, kv_send.at[0, l, c], kv_recv.at[0, l, c], device)
+        @pl.when(l == 0)
+        def _():
+            pass_on((1, 2, 3), 0)
+            pass_on((0, 1, 2, 3), 1)
+
         for device in gx_peers:
             block = qg.at[l, :, gx]
             put(block, block, kv_send.at[1, l, 0], kv_recv.at[1, l, 0], device)
 
-        @pl.when(l == 0)
-        def _():
-            pass_on((1, 2, 3), 0)
-
         @pl.when(l == 1)
         def _():
             for c in range(2):
                 start_gradient(1, c)
 
+        later = []
         for c in range(2):
             wait_bytes(kv.at[l, :, c, 0:7], kv_recv.at[0, l, c])
             all_keys = kv[l, 0, c].reshape(640, LANES)
@@ -353,6 +366,9 @@
             if c == 0:
                 wait_weights(1, l)
             scatter_gy(dot_nn(mixed_low, by_columns(wo, l)), K_O, l, c)
+            later.append((c, full, weights, mixed, all_values, highest, summed))
+
+        for c, full, weights, mixed, all_values, highest, summed in later:
             left_out = (full - weights.astype(F32)).astype(BF)
             attn_f[l, image_rows(c)] = mixed + join_heads(dot_nn(left_out, all_values))
             logs = highest + jnp.log(summed)
@@ -362,20 +378,13 @@
                     line = jnp.where(lane_id == head * 3 + at, piece, line)
             aux[l, image_rows(c)] = line
 
-        @pl.when(l == 0)
-        def _():
-            pass_on((0, 1), 1)
-
         for c in range(2):
             middle = res[image_rows(c)] + wait_scatter(K_O, l, c) + vec[l, V_BO, :, mine]
             mid[image_rows(c)] = middle
             mg[l, image_rows(c), mine] = middle.astype(BF)
             gather_gy(mg, K_M, l, c)
 
-        @pl.when(l == 0)
-        def _():
-            pass_on((2, 3), 1)
-
+        slopes = []
         bias = jnp.concatenate([vec[l, V_BU + n, :, mine] for n in range(4)], axis=1)
         for c in range(2):
             wait_gather(mg, K_M, l, c)
@@ -389,6 +398,9 @@
             if c == 0:
                 wait_weights(3, l)
             scatter_gy(dot_nn(hidden, by_columns(wdn, l)), K_D, l, c)
+            slopes.append((pre_act, gate))
+
+        for c, (pre_act, gate) in enumerate(slopes):
             slope = jnp.exp(-0.5 * pre_act * pre_act) * 0.3989422804014327
             pre[l, image_rows(c)] = gate + pre_act * slope
 
@@ -696,6 +708,40 @@
     g_w_down[...] = final_sum(3)
     g_w_up[...] = final_sum(2)
     g_w_out[...] = final_sum(1)
+    wait_bytes(ybuf.at[0], a_send.at[0])
+    wait_bytes(igbuf.at[0], i_send.at[0])
+    wait_bytes(vec.at[s, :, :, 0:896], vec_send.at[0])
+    wait_bytes(vec.at[s], vec_send.at[1])
+    for group in range(4):
+        ref = weights_at[group]
+        first, _ = halves(group)
+        wait_bytes(ref.at[0, 0:3, 0, first], wa1_send.at[group])
+        wait_bytes(ref.at[0, 0:3, 0, first], wb1_send.at[group])
+        wait_bytes(ref.at[0, 0:3], wa2_send.at[group])
+        wait_bytes(rb2[group].at[0:3], gb2_send.at[group])
+        for l in range(2):
+            wait_bytes(ref.at[0, 0:3, :, first], wb2_send.at[group, l])
+            wait_bytes(ra1[group].at[l, 0:3], ga1_send.at[group, l])
+    for l in range(2):
+        for c in range(2):
+            for kind, buffer in ((K_X, xg), (K_M, mg), (K_G, gg), (K_GM, gmg)):
+                wait_bytes(buffer.at[l, image_rows(c), 0:896], gy_send.at[kind, l, c])
+            for kind, slot in slot_of.items():
+                wait_bytes(rsb.at[slot, l, c, 0:7], gy_send.at[kind, l, c])
+            for which in range(2):
+                wait_bytes(stat.at[which, l, c, 0:7], st_send.at[which, l, c])
+            wait_bytes(kv.at[l, :, c, 0:7], kv_send.at[0, l, c])
+            wait_bytes(dog.at[l, c, 0:7], do_send.at[l, c])
+        wait_bytes(qg.at[l, :, 0:7], kv_send.at[1, l, 0])
+        for count, at in ((1, l), (2, 1 - l)):
+
+            @pl.when(s == at)
+            def _(l=l, count=count):
+                for group in range(4):
+                    wait_bytes(ra2[group].at[0:count], ga2_send.at[group, l])
+                    wait_bytes(rb1[group].at[0:count], gb1_send.at[group, l])
+                wait_bytes(r_vec.at[0 : 6 + count], v_send.at[l])
+
     total = final_sum(0)
     g_w_query[...] = total[:, :LANES]
     g_w_key[...] = total[:, LANES : 2 * LANES]
@@ -714,40 +760,6 @@
         g_b_up[:, part * LANES : (part + 1) * LANES] = total[V_BU + part]
     wait_bytes(act_o, a_recv.at[0])
     wait_bytes(ig_o, i_recv.at[0])
-
-    wait_bytes(ybuf.at[0], a_send.at[0])
-    wait_bytes(igbuf.at[0], i_send.at[0])
-    wait_bytes(vec.at[s, :, :, 0:896], vec_send.at[0])
-    wait_bytes(vec.at[s], vec_send.at[1])
-    for group in range(4):
-        ref = weights_at[group]
-        first, _ = halves(group)
-        wait_bytes(ref.at[0, 0:3, 0, first], wa1_send.at[group])
-        wait_bytes(ref.at[0, 0:3, 0, first], wb1_send.at[group])
-        wait_bytes(ref.at[0, 0:3], wa2_send.at[group])
-        wait_bytes(rb2[group].at[0:3], gb2_send.at[group])
-        for l in range(2):
-            wait_bytes(ref.at[0, 0:3, :, first], wb2_send.at[group, l])
-            wait_bytes(ra1[group].at[l, 0:3], ga1_send.at[group, l])
-    for l in range(2):
-        for c in range(2):
-            for kind, buffer in ((K_X, xg), (K_M, mg), (K_G, gg), (K_GM, gmg)):
-                wait_bytes(buffer.at[l, image_rows(c), 0:896], gy_send.at[kind, l, c])
-            for kind, slot in slot_of.items():
-                wait_bytes(rsb.at[slot, l, c, 0:7], gy_send.at[kind, l, c])
-            for which in range(2):
-                wait_bytes(stat.at[which, l, c, 0:7], st_send.at[which, l, c])
-            wait_bytes(kv.at[l, :, c, 0:7], kv_send.at[0, l, c])
-            wait_bytes(dog.at[l, c, 0:7], do_send.at[l, c])
-        wait_bytes(qg.at[l, :, 0:7], kv_send.at[1, l, 0])
-        for count, at in ((1, l), (2, 1 - l)):
-
-            @pl.when(s == at)
-            def _(l=l, count=count):
-                for group in range(4):
-                    wait_bytes(ra2[group].at[0:count], ga2_send.at[group, l])
-                    wait_bytes(rb1[group].at[0:count], gb1_send.at[group, l])
-                wait_bytes(r_vec.at[0 : 6 + count], v_send.at[l])
 
 
 def write_out(*refs):

time: 195 us -> 190 us (0.974)
  Pallas kernels: 194 us -> 189 us
    pallas_call x1, Pallas kernels: 191 us -> 187 us  [local(): pl.pallas_call(kernel, out_shape=out_shape, in_specs=in_specs, out_specs=...]
where the time goes in v4:
time: 190 us
  Pallas kernels  189 us (99%)
    pallas_call x1, Pallas kernels, local(): pl.pallas_call(kernel, out_shape=out_shape, in_specs=in_specs, out_specs=...  187 us

profile of v4, /device:TPU:1, one launch (start us, length us, event | category | flops | bytes accessed | tf_op | source)
XLA Modules:
  0.0 189.9 jit_solution(863856136368142885)
XLA Ops:
  0.7 186.8 %two_sections.1 = (bf16[2,160,128]{2,1,0:T(8,128)(2,1)}, f32[2,160,128]{2,1,0:T(8,128)}, f32[1,128]{1,0:T(1,128)}, f32[1,128]{1,0:T(1,128)}, f32[128,128]{1,0:T(...) custom-call(bf16[2,160,128]{2,1,0:T(8,128)(2,1)} %bitcast.21, ...), custom_call_target="tpu_custom_call" | custom-call | flops 4000000000 | bytes 8000000 | tf_op jit(solution)/shard_map/two_sections/pallas_call | solution.py:883
  187.5 2.4 %write_results.1 = (bf16[2,160,128]{2,1,0:T(8,128)(2,1)}, f32[2,160,128]{2,1,0:T(8,128)}, f32[1,128]{1,0:T(1,128)}, f32[1,128]{1,0:T(1,128)}, f32[128,128]{1,0:T...) custom-call(bf16[2,160,128]{2,1,0:T(8,128)(2,1)} %get-tuple-element., ...), custom_call_target="tpu_custom_call" | custom-call | tf_op jit(solution)/shard_map/write_results/pallas_call | solution.py:776
